TPU v7x, 512 devices: a whole 4x4x16 slice. The times are simulated.
512 devices in a mesh: rep: 32 (over z_lo, x), tp: 16 (over y, z_hi, core).
Axes of the slice: x: 4, y: 4, z: 16 (z_hi: 2, z_lo: 8; z = z_hi * 8 + z_lo), core: 2. Of those that a mesh axis runs over, the one named last changes fastest.
Arguments:
- quant_codes: int32 [32, 32, 49152], P('rep', None, 'tp'), may hold values from 0 to 15
- block_scales: float32 [32, 32, 384], P('rep', None, 'tp'), may hold values from 0.02 to 0.2
- outer_params: float32 [32, 49152], P(None, 'tp'), may hold values from -3 to 3
- outer_moment: float32 [32, 49152], P('rep', 'tp'), may hold values from -0.3 to 0.3
- inputs: bfloat16 [8192, 128], P('rep'), may hold values from -6 to 6
- saved_pre: bfloat16 [8192, 49152], P('rep', 'tp'), may hold values from -8 to 8
- grad_out: bfloat16 [8192, 49152], P('rep', 'tp'), may hold values from -0.375 to 0.375
- weights: bfloat16 [32, 128, 49152], P('rep', None, 'tp'), may hold values from -0.5 to 0.5
Outputs:
- new_params: float32 [32, 49152], P(None, 'tp')
- new_moment: float32 [32, 49152], P('rep', 'tp')
- weight_grad: bfloat16 [32, 128, 49152], P('rep', None, 'tp')
- input_grad_t: bfloat16 [128, 8192], P('tp', 'rep')
All inputs are finite; a program needn't handle non-finite values.
Results may differ from a plain program's by a relative error of at most 0.0048.
Values sent between devices are 32-bit elements; how exact they have to be, the bound alone decides.
No kernel may reach another device: no remote copies, remote signals or barrier semaphores. Data moves between devices by JAX's collectives and lax.ppermute only.
A program may use at most 64 MiB of HBM per device.

v0:
```python
import jax
import jax.numpy as jnp
from jax import lax
from jax.sharding import PartitionSpec as P

outer_rate = 0.7
outer_momentum = 0.9
slope_scale = 0.7978845608028654


def gelu_slope(values):
    cubed_values = values * values * values
    tanh_term = jnp.tanh(slope_scale * (values + 0.044715 * cubed_values))
    return 0.5 * (1.0 + tanh_term) + 0.5 * values * (1.0 - tanh_term * tanh_term) * slope_scale * (
        1.0 + 0.134145 * values * values
    )


def on_device(
    quant_codes, block_scales, outer_params, outer_moment, inputs, saved_pre, grad_out, weights
):
    pre_grad = (grad_out.astype(jnp.float32) * gelu_slope(saved_pre.astype(jnp.float32))).astype(
        jnp.bfloat16
    )
    weight_sheet = weights[0]
    weight_grad = lax.dot_general(
        inputs, pre_grad, (((0,), (0,)), ((), ())), preferred_element_type=jnp.float32
    ).astype(jnp.bfloat16)[None]
    input_grad_t = lax.psum_scatter(
        lax.dot_general(
            weight_sheet, pre_grad, (((1,), (1,)), ((), ())), preferred_element_type=jnp.float32
        ),
        "tp",
        scatter_dimension=0,
        tiled=True,
    ).astype(jnp.bfloat16)
    groups = lax.axis_size("rep")
    slab_rows = quant_codes.shape[1]
    centred = quant_codes[0].astype(jnp.float32) - 7.5
    blocked = centred.reshape(slab_rows, block_scales.shape[2], -1) * block_scales[0][:, :, None]
    pseudo_grad = blocked.reshape(slab_rows, -1)
    owned_rows = outer_moment.shape[0]
    offset = lax.axis_index("rep") * owned_rows
    average = lax.psum(pseudo_grad, "rep") / groups
    whole_moment = lax.all_gather(outer_moment, "rep", axis=0, tiled=True)
    full_moment = outer_momentum * whole_moment + average
    new_params = outer_params - outer_rate * (average + outer_momentum * full_moment)
    new_moment = lax.dynamic_slice_in_dim(full_moment, offset, owned_rows, 0)
    return (new_params, new_moment, weight_grad, input_grad_t)


def solution(mesh):
    in_specs = (
        P("rep", None, "tp"),
        P("rep", None, "tp"),
        P(None, "tp"),
        P("rep", "tp"),
        P("rep", None),
        P("rep", "tp"),
        P("rep", "tp"),
        P("rep", None, "tp"),
    )
    out_specs = (P(None, "tp"), P("rep", "tp"), P("rep", None, "tp"), P("tp", "rep"))
    return jax.shard_map(
        on_device, mesh=mesh, in_specs=in_specs, out_specs=out_specs, check_vma=False
    )
```

profile of v0, /device:TPU:8, one launch (start us, length us, event | category | flops | bytes accessed | tf_op | source)
XLA Modules:
  0.0 471.7 jit_solution(517255833558885080)
XLA Ops:
  8.0 0.0 copy-start
  8.0 0.0 reduce-scatter.4.cloned.1.call-start
  8.1 3.7 fusion.9
  11.7 0.0 copy-done
  11.7 0.0 copy-start.4
  11.7 0.0 copy-start.1
  11.8 0.6 convolution_bitcast_fusion
  12.3 0.0 copy-start.3
  12.3 0.8 copy.18
  13.1 0.0 reduce-scatter.4.cloned.1.call-update
  13.1 0.0 all-reduce.2.cloned.1.call-start
  13.2 0.0 copy-done.4
  13.2 0.1 copy.15
  13.3 0.2 mul.71
  13.4 0.0 copy-done.1
  13.4 0.8 bitcast_multiply_fusion
  14.3 0.0 all-reduce.2.cloned.1.call-update
  14.3 0.0 copy-done.3
  14.3 126.8 %all-gather = f32[32,1,3072]{2,1,0:T(1,128)S(1)} all-gather(f32[1,1,3072]{2,1,0:T(1,128)S(1)} %bitcast.25), channel_id=1, replica_groups=mesh['rep'=32,'tp'=16] {'rep'}, dimensions={0}, use_global_device_ids=true | all-gather | bytes 405504 | tf_op jit(solution)/shard_map/all_gather | solution.py:45
  141.1 1.5 fusion
  142.5 0.0 copy-start.2
  142.5 1.2 copy.16
  143.7 0.4 broadcast_multiply_fusion
  144.1 0.0 reduce-scatter.4.cloned.1.call-done
  144.1 0.8 copy.19
  145.0 0.7 copy.17
  145.6 316.2 %all-reduce.2.cloned.1.call-done = f32[32,3072]{1,0:T(8,128)} async-done(((f32[32,3072]{1,0:T(8,128)}), f32[32,3072]{1,0:T(8,128)}) %all-reduce.2.cloned.1.call-update) | async-done | bytes 393232 | tf_op jit(solution)/shard_map/psum | solution.py:44
  461.8 0.0 copy-done.2
  461.8 1.9 bitcast_add_fusion
  463.7 0.6 constant_dynamic-slice_fusion
Async XLA Ops:
  8.0 3.7 copy-start
  8.0 136.1 %reduce-scatter.4.cloned.1.call-start = ((), (), s32[]{:S(2)}) async-start(), calls=%async_computation.2 | async-start | bytes 139264
  11.7 1.4 copy-start.4
  11.7 1.7 copy-start.1
  12.3 2.0 copy-start.3
  13.1 448.7 %all-reduce.2.cloned.1.call-start = ((), (), s32[]{:S(2)}) async-start(), calls=%async_computation.1 | async-start | bytes 786432 | tf_op jit(solution)/shard_map/psum | solution.py:44
  142.5 319.3 %copy-start.2 = (f32[32,3072]{1,0:T(8,128)S(1)}, f32[32,3072]{1,0:T(8,128)}, u32[]{:S(2)}) copy-start(f32[32,3072]{1,0:T(8,128)} %param.10) | copy-start | bytes 1179652
Sparse Core Ops, SparseCore 0:
  14.1 100.0 reduce-scatter.3
Sparse Core Ops, SparseCore 1:
  17.1 444.7 all-reduce.1
where the time goes:
time: 472 us
  waiting for transfers between devices  316 us (67%)
  blocking collectives  127 us (27%)
  between operations  15.6 us (3%)
  other arithmetic  6.78 us (1%)
    psum x1, waiting for transfers between devices, on_device(): average = lax.psum(pseudo_grad, 'rep') / groups  316 us
    all_gather x1, blocking collectives, on_device(): whole_moment = lax.all_gather(outer_moment, 'rep', axis=0, tiled=True)  127 us
  transfers between devices with their start and end apart: 2, of which 1 were waited for; matrix products, arithmetic and copies ran while one was open for 1% of the time, Pallas kernels for 0%

commit v1 on v0

v1 whole, which is shorter than its diff:
```python
import functools

import jax
import jax.numpy as jnp
from jax import lax
from jax.experimental import pallas as pl
from jax.experimental.pallas import tpu as pltpu
from jax.sharding import PartitionSpec as P

outer_rate = 0.7
outer_momentum = 0.9
slope_scale = 0.7978845608028654
carry = outer_momentum * outer_momentum / (1.0 + outer_momentum)
param_step = outer_rate * (1.0 + outer_momentum)
moment_rest = outer_momentum - carry
near = 8
block = 128


def full(shape):
    return pl.BlockSpec(shape, lambda *_: (0,) * len(shape))


def dequant_kernel(codes_ref, scales_ref, moment_ref, out_ref, *, groups):
    parts, rows, width = out_ref.shape
    own = lax.broadcasted_iota(jnp.int32, (rows, block), 0) == lax.axis_index("rep")
    for j in range(parts * width // block):
        cols = slice(j * block, (j + 1) * block)
        grads = (codes_ref[0, :, cols].astype(jnp.float32) - 7.5) * (
            scales_ref[0, :, j : j + 1] * (1.0 / groups)
        )
        kept = jnp.where(own, carry * moment_ref[:, cols], 0.0)
        part, at = divmod(j * block, width)
        out_ref[part, :, at : at + block] = grads + kept


def backward_kernel(
    inputs_ref, pre_ref, grad_ref, weights_ref, wgrad_ref, keep_ref, send_ref, total
):
    step = pl.program_id(0)

    @pl.when(step == 0)
    def _():
        total[...] = jnp.zeros_like(total)

    v = pre_ref[...].astype(jnp.float32)
    u = v * v
    t = jnp.tanh(v * (slope_scale + (slope_scale * 0.044715) * u))
    slope = (0.5 + 0.5 * t) * (
        1.0 + (v * (slope_scale + (slope_scale * 0.134145) * u)) * (1.0 - t)
    )
    pre_grad = (grad_ref[...].astype(jnp.float32) * slope).astype(jnp.bfloat16)
    wgrad_ref[0] = lax.dot_general(
        inputs_ref[...], pre_grad, (((0,), (0,)), ((), ())), preferred_element_type=jnp.float32
    ).astype(jnp.bfloat16)
    total[...] += lax.dot_general(
        weights_ref[0], pre_grad, (((1,), (1,)), ((), ())), preferred_element_type=jnp.float32
    ).reshape(total.shape)

    @pl.when(step == pl.num_programs(0) - 1)
    def _():
        core = lax.axis_index("tp") % 2
        for j in range(keep_ref.shape[0]):
            keep_ref[j] = total[2 * j + core]
            send_ref[j] = total[2 * j + 1 - core]


def halve_kernel(kept_ref, came_ref, keep_ref, send_ref, *, bit):
    half = keep_ref.shape[0]
    side = (lax.axis_index("tp") // bit) % 2
    for out_ref, at in ((keep_ref, side * half), (send_ref, (1 - side) * half)):
        out_ref[...] = kept_ref[pl.ds(at, half)] + came_ref[pl.ds(at, half)]


def join_kernel(kept_ref, came_ref, out_ref):
    out_ref[...] = (kept_ref[0] + came_ref[0]).astype(out_ref.dtype)


def outer_kernel(sums_ref, params_ref, moment_ref, params_out_ref, moment_out_ref):
    parts, _, width = sums_ref.shape
    own = lax.axis_index("rep")
    for part in range(parts):
        cols = slice(part * width, (part + 1) * width)
        params_out_ref[:, cols] = params_ref[:, cols] - param_step * sums_ref[part]
        moment_out_ref[:, cols] = (
            sums_ref[part, pl.ds(own, 1), :] + moment_rest * moment_ref[:, cols]
        )


def swap(array, axis, bit):
    size = lax.axis_size(axis)
    return lax.ppermute(array, axis, [(i, i ^ bit) for i in range(size)])


def halve(kept, came, bit):
    half = kept.shape[0] // 2
    part = jax.ShapeDtypeStruct((half,) + kept.shape[1:], jnp.float32)
    return pl.pallas_call(
        functools.partial(halve_kernel, bit=bit), out_shape=(part, part), name=f"halve{bit}"
    )(kept, came)


def on_device(
    quant_codes, block_scales, outer_params, outer_moment, inputs, saved_pre, grad_out, weights
):
    groups = lax.axis_size("rep")
    _, rows, hidden = quant_codes.shape
    tokens, window = inputs.shape
    width = hidden // near
    near_groups = [list(range(i, i + near)) for i in range(0, groups, near)]

    parts = pl.pallas_call(
        functools.partial(dequant_kernel, groups=groups),
        out_shape=jax.ShapeDtypeStruct((near, rows, width), jnp.float32),
        name="dequant",
    )(quant_codes, block_scales, outer_moment)
    parts = lax.all_to_all(parts, "rep", 0, 0, axis_index_groups=near_groups, tiled=True)
    chunk = jnp.sum(parts, axis=0)

    tile = 512
    shares = lax.axis_size("tp")
    half = jax.ShapeDtypeStruct((shares // 2, window // shares, tokens), jnp.float32)
    weight_grad, keep, send = pl.pallas_call(
        backward_kernel,
        grid=(hidden // tile,),
        in_specs=[
            full((tokens, window)),
            pl.BlockSpec((tokens, tile), lambda i: (0, i)),
            pl.BlockSpec((tokens, tile), lambda i: (0, i)),
            pl.BlockSpec((1, window, tile), lambda i: (0, 0, i)),
        ],
        out_specs=[
            pl.BlockSpec((1, window, tile), lambda i: (0, 0, i)),
            full(half.shape),
            full(half.shape),
        ],
        out_shape=(jax.ShapeDtypeStruct((1, window, hidden), jnp.bfloat16), half, half),
        scratch_shapes=[pltpu.VMEM((shares, window // shares, tokens), jnp.float32)],
        cost_estimate=pl.CostEstimate(
            flops=4 * tokens * window * hidden,
            bytes_accessed=4 * tokens * hidden + 4 * window * hidden,
            transcendentals=tokens * hidden,
        ),
        name="backward",
    )(inputs, saved_pre, grad_out, weights)

    chunk = chunk + swap(chunk, "rep", near)
    came = swap(send, "tp", 1)
    keep, send = halve(keep, came, 8)
    came = swap(send, "tp", 8)
    keep, send = halve(keep, came, 4)
    came = swap(send, "tp", 4)
    keep, send = halve(keep, came, 2)
    came = swap(send, "tp", 2)
    input_grad_t = pl.pallas_call(
        join_kernel,
        out_shape=jax.ShapeDtypeStruct((window // shares, tokens), jnp.bfloat16),
        name="join",
    )(keep, came)
    chunk = chunk + swap(chunk, "rep", 2 * near)

    sums = lax.all_to_all(
        jnp.broadcast_to(chunk, (near,) + chunk.shape),
        "rep",
        0,
        0,
        axis_index_groups=near_groups,
        tiled=True,
    )
    new_params, new_moment = pl.pallas_call(
        outer_kernel,
        out_shape=(
            jax.ShapeDtypeStruct(outer_params.shape, jnp.float32),
            jax.ShapeDtypeStruct(outer_moment.shape, jnp.float32),
        ),
        name="outer_step",
    )(sums, outer_params, outer_moment)
    return (new_params, new_moment, weight_grad, input_grad_t)


def solution(mesh):
    in_specs = (
        P("rep", None, "tp"),
        P("rep", None, "tp"),
        P(None, "tp"),
        P("rep", "tp"),
        P("rep", None),
        P("rep", "tp"),
        P("rep", "tp"),
        P("rep", None, "tp"),
    )
    out_specs = (P(None, "tp"), P("rep", "tp"), P("rep", None, "tp"), P("tp", "rep"))
    return jax.shard_map(
        on_device, mesh=mesh, in_specs=in_specs, out_specs=out_specs, check_vma=False
    )
```

time: 472 us -> 92.8 us (0.20)
  the two profiles are of different devices: /device:TPU:8 before, /device:TPU:26 now
where the time goes in v1:
time: 92.8 us; the launch traced here: 92 us
  starting transfers between devices  40.7 us (44%)
  waiting for transfers between devices  16 us (17%)
  Pallas kernels  15.8 us (17%)
  blocking collectives  13.3 us (14%)
  local copies, waits for them, and re-layouts  5.32 us (6%)
    ppermute x6, starting transfers between devices, swap(): return lax.ppermute(array, axis, [(i, i ^ bit) for i in range(size)])  36.2 us
    ppermute x6, waiting for transfers between devices, swap(): return lax.ppermute(array, axis, [(i, i ^ bit) for i in range(size)])  16 us
    all_to_all x1, blocking collectives, on_device(): lax.all_to_all(parts, 'rep', 0, 0, axis_index_groups=near_groups, tiled=T...  13.3 us
    pallas_call x1, Pallas kernels, on_device(): pl.pallas_call(backward_kernel, grid=(hidden // tile,), in_specs=[full((t...  6.44 us
    unnamed x11, local copies, waits for them, and re-layouts  4.55 us
    all_to_all x1, starting transfers between devices, on_device(): lax.all_to_all(jnp.broadcast_to(chunk, (near,) + chunk.shape), 'rep', 0,...  4.53 us
    pallas_call x3, Pallas kernels, halve(): pl.pallas_call(functools.partial(halve_kernel, bit=bit), out_shape=(part,...  4.22 us
    pallas_call x1, Pallas kernels, on_device(): pl.pallas_call(functools.partial(dequant_kernel, groups=groups), out_shap...  1.97 us
  transfers between devices with their start and end apart: 7, of which 6 were waited for; matrix products, arithmetic and copies ran while one was open for 0% of the time, Pallas kernels for 13%

profile of v1, /device:TPU:26, one launch (start us, length us, event | category | flops | bytes accessed | tf_op | source)
XLA Modules:
  0.0 92.0 jit_solution(11018847317011004664)
XLA Ops:
  0.6 1.4 %copy.12.scales_ref = f32[1,32,24]{2,1,0:T(8,128)} copy(f32[1,32,24]{1,2,0:T(8,128)} %param.9) | data formatting | bytes 6144 | tf_op args[1]
  2.0 2.0 %dequant.1 = f32[8,32,384]{2,1,0:T(8,128)} custom-call(s32[1,32,3072]{2,1,0:T(8,128)} %codes_ref.1, f32[1,32,24]{2,1,0:T(8,128)} %copy.12.scales_ref, f32[1,3072]{1,0:T(1,128)} %moment_ref.3), custom_call_target="tpu_custom_call" | custom-call | tf_op jit(solution)/shard_map/dequant/pallas_call | solution.py:112
  4.0 13.3 %all_to_all.10 = f32[8,32,384]{2,1,0:T(8,128)S(1)} all-to-all(f32[8,32,384]{2,1,0:T(8,128)} %dequant.1), channel_id=1, replica_groups={{0,16,32,48,64,80,96,112},{128,144,160,176,192,208,224,240},{256,272,28..., dimensions={0} | all-to-all | bytes 786432 | tf_op jit(solution)/shard_map/all_to_all | solution.py:117
  17.4 5.2 %collective-permute-start = (f32[32,384]{1,0:T(8,128)S(1)}, f32[32,384]{1,0:T(8,128)S(1)}, u32[]{:S(2)}, u32[]{:S(2)}) collective-permute-start(f32[32,384]{1,0:T(8,128)S(1)} %reduce_sum.9), channel_id=1, source_target_pairs={{0,128},{16,144},{32,160},{48,176},{64,192},{80,208},{96,224},{112... | collective-permute-start | bytes 147464 | tf_op jit(solution)/shard_map/ppermute | solution.py:92
  22.5 2.6 %collective-permute-done = f32[32,384]{1,0:T(8,128)S(1)} collective-permute-done((f32[32,384]{1,0:T(8,128)S(1)}, f32[32,384]{1,0:T(8,128)S(1)}, u32[]{:S(2)}, u32[]{:S(2)}) %collective-permute-start) | collective-permute-done | bytes 49184 | tf_op jit(solution)/shard_map/ppermute | solution.py:92
  25.1 9.1 %collective-permute-start.1 = (f32[32,384]{1,0:T(8,128)S(1)}, f32[32,384]{1,0:T(8,128)S(1)}, u32[]{:S(2)}, u32[]{:S(2)}) collective-permute-start(f32[32,384]{1,0:T(8,128)S(1)} %add.6), channel_id=1, source_target_pairs={{0,256},{16,272},{32,288},{48,304},{64,320},{80,336},{96,352},{112... | collective-permute-start | bytes 147464 | tf_op jit(solution)/shard_map/ppermute | solution.py:92
  34.2 2.6 %collective-permute-done.1 = f32[32,384]{1,0:T(8,128)S(1)} collective-permute-done((f32[32,384]{1,0:T(8,128)S(1)}, f32[32,384]{1,0:T(8,128)S(1)}, u32[]{:S(2)}, u32[]{:S(2)}) %collective-permute-start.1) | collective-permute-done | bytes 49184 | tf_op jit(solution)/shard_map/ppermute | solution.py:92
  36.9 0.8 broadcast_in_dim.3
  37.6 4.5 %all-to-all-start.1 = ((f32[8,32,384]{2,1,0:T(8,128)}), f32[8,32,384]{2,1,0:T(8,128)S(1)}, u32[]{:S(2)}, u32[]{:S(2)}) async-start(f32[8,32,384]{2,1,0:T(8,128)} %broadcast_in_dim.3), calls=%async_computation.1 | async-start | bytes 786432 | tf_op jit(solution)/shard_map/all_to_all | solution.py:162
  42.2 6.4 %backward.1 = (bf16[1,128,3072]{2,1,0:T(8,128)(2,1)}, f32[8,8,256]{2,1,0:T(8,128)}, f32[8,8,256]{2,1,0:T(8,128)}) custom-call(bf16[256,128]{1,0:T(8,128)(2,1)} %inputs_ref.1, bf16[256,3072]{1,0:T(8,128)(2,1)} %pre_ref.1, bf16[256,3072]{1,0:T(8,128)(2,1)} %grad_ref.1, bf16[1,128,3072]{2,1,0:T(8,128)(2,1)} %weights_ref.1), custom_call_target="tpu_custom_call" | custom-call | flops 402653184 | bytes 4718592 | tf_op jit(solution)/shard_map/backward/pallas_call | solution.py:123
  48.6 1.9 %collective-permute-start.2 = (f32[8,8,256]{2,1,0:T(8,128)}, f32[8,8,256]{2,1,0:T(8,128)S(1)}, u32[]{:S(2)}, u32[]{:S(2)}) collective-permute-start(f32[8,8,256]{2,1,0:T(8,128)} %get-tuple-element.19), channel_id=1, source_target_pairs={{0,1},{1,0},{2,3},{3,2},{4,5},{5,4},{6,7},{7,6},{8,9},{9,8},{10,11... | collective-permute-start | bytes 196616 | tf_op jit(solution)/shard_map/ppermute | solution.py:92
  50.5 1.4 %collective-permute-done.2.came_ref = f32[8,8,256]{2,1,0:T(8,128)S(1)} collective-permute-done((f32[8,8,256]{2,1,0:T(8,128)}, f32[8,8,256]{2,1,0:T(8,128)S(1)}, u32[]{:S(2)}, u32[]{:S(2)}) %collective-permute-start.2) | collective-permute-done | bytes 65568 | tf_op jit(solution)/shard_map/ppermute | solution.py:92
  52.0 0.0 copy-start.1
  52.0 0.6 copy-done.1
  52.6 1.5 %halve8.1 = (f32[4,8,256]{2,1,0:T(8,128)}, f32[4,8,256]{2,1,0:T(8,128)}) custom-call(f32[8,8,256]{2,1,0:T(8,128)} %get-tuple-element.18.kept_ref, f32[8,8,256]{2,1,0:T(8,128)} %copy-done.1), custom_call_target="tpu_custom_call" | custom-call | tf_op jit(solution)/shard_map/halve8/pallas_call | solution.py:98
  54.1 3.1 %collective-permute-start.3 = (f32[4,8,256]{2,1,0:T(8,128)}, f32[4,8,256]{2,1,0:T(8,128)S(1)}, u32[]{:S(2)}, u32[]{:S(2)}) collective-permute-start(f32[4,8,256]{2,1,0:T(8,128)} %get-tuple-element.21), channel_id=1, source_target_pairs={{0,8},{1,9},{2,10},{3,11},{4,12},{5,13},{6,14},{7,15},{8,0},{9,1},... | collective-permute-start | bytes 98312 | tf_op jit(solution)/shard_map/ppermute | solution.py:92
  57.2 4.4 %collective-permute-done.3.came_ref = f32[4,8,256]{2,1,0:T(8,128)S(1)} collective-permute-done((f32[4,8,256]{2,1,0:T(8,128)}, f32[4,8,256]{2,1,0:T(8,128)S(1)}, u32[]{:S(2)}, u32[]{:S(2)}) %collective-permute-start.3) | collective-permute-done | bytes 32800 | tf_op jit(solution)/shard_map/ppermute | solution.py:92
  61.6 0.0 copy-start.2
  61.6 0.6 copy-done.2
  62.2 1.4 %halve4.1 = (f32[2,8,256]{2,1,0:T(8,128)}, f32[2,8,256]{2,1,0:T(8,128)}) custom-call(f32[4,8,256]{2,1,0:T(8,128)} %get-tuple-element.20.kept_ref, f32[4,8,256]{2,1,0:T(8,128)} %copy-done.2), custom_call_target="tpu_custom_call" | custom-call | tf_op jit(solution)/shard_map/halve4/pallas_call | solution.py:98
  63.6 2.6 %collective-permute-start.4 = (f32[2,8,256]{2,1,0:T(8,128)}, f32[2,8,256]{2,1,0:T(8,128)S(1)}, u32[]{:S(2)}, u32[]{:S(2)}) collective-permute-start(f32[2,8,256]{2,1,0:T(8,128)} %get-tuple-element.23), channel_id=1, source_target_pairs={{0,4},{1,5},{2,6},{3,7},{4,0},{5,1},{6,2},{7,3},{8,12},{9,13},{10,... | collective-permute-start | bytes 49160 | tf_op jit(solution)/shard_map/ppermute | solution.py:92
  66.2 3.2 %collective-permute-done.4.came_ref = f32[2,8,256]{2,1,0:T(8,128)S(1)} collective-permute-done((f32[2,8,256]{2,1,0:T(8,128)}, f32[2,8,256]{2,1,0:T(8,128)S(1)}, u32[]{:S(2)}, u32[]{:S(2)}) %collective-permute-start.4) | collective-permute-done | bytes 16416 | tf_op jit(solution)/shard_map/ppermute | solution.py:92
  69.4 0.0 copy-start.3
  69.4 0.6 copy-done.3
  70.0 1.3 %halve2.1 = (f32[1,8,256]{2,1,0:T(8,128)}, f32[1,8,256]{2,1,0:T(8,128)}) custom-call(f32[2,8,256]{2,1,0:T(8,128)} %get-tuple-element.22.kept_ref, f32[2,8,256]{2,1,0:T(8,128)} %copy-done.3), custom_call_target="tpu_custom_call" | custom-call | tf_op jit(solution)/shard_map/halve2/pallas_call | solution.py:98
  71.3 14.2 %collective-permute-start.5 = (f32[1,8,256]{2,1,0:T(8,128)}, f32[1,8,256]{2,1,0:T(8,128)S(1)}, u32[]{:S(2)}, u32[]{:S(2)}) collective-permute-start(f32[1,8,256]{2,1,0:T(8,128)} %get-tuple-element.25), channel_id=1, source_target_pairs={{0,2},{1,3},{2,0},{3,1},{4,6},{5,7},{6,4},{7,5},{8,10},{9,11},{10,... | collective-permute-start | bytes 24584 | tf_op jit(solution)/shard_map/ppermute | solution.py:92
  85.6 1.8 %collective-permute-done.5.came_ref = f32[1,8,256]{2,1,0:T(8,128)S(1)} collective-permute-done((f32[1,8,256]{2,1,0:T(8,128)}, f32[1,8,256]{2,1,0:T(8,128)S(1)}, u32[]{:S(2)}, u32[]{:S(2)}) %collective-permute-start.5) | collective-permute-done | bytes 8224 | tf_op jit(solution)/shard_map/ppermute | solution.py:92
  87.4 0.0 copy-start.4
  87.4 0.6 copy-done.4
  88.0 1.3 %join.1 = bf16[8,256]{1,0:T(8,128)(2,1)} custom-call(f32[1,8,256]{2,1,0:T(8,128)} %get-tuple-element.24.kept_ref, f32[1,8,256]{2,1,0:T(8,128)} %copy-done.4), custom_call_target="tpu_custom_call" | custom-call | tf_op jit(solution)/shard_map/join/pallas_call | solution.py:155
  89.3 0.0 all-to-all-done.1.sums_ref
  89.3 0.0 copy-start
  89.3 0.7 copy-done
  90.1 1.9 %outer_step.1 = (f32[32,3072]{1,0:T(8,128)}, f32[1,3072]{1,0:T(1,128)}) custom-call(f32[8,32,384]{2,1,0:T(8,128)} %copy-done, f32[32,3072]{1,0:T(8,128)} %params_ref.1, f32[1,3072]{1,0:T(1,128)} %moment_ref.3), custom_call_target="tpu_custom_call" | custom-call | tf_op jit(solution)/shard_map/outer_step/pallas_call | solution.py:170
  (3 shorter events, 0.0 us)
Async XLA Ops:
  17.4 7.8 %collective-permute-start = (f32[32,384]{1,0:T(8,128)S(1)}, f32[32,384]{1,0:T(8,128)S(1)}, u32[]{:S(2)}, u32[]{:S(2)}) collective-permute-start(f32[32,384]{1,0:T(8,128)S(1)} %reduce_sum.9), channel_id=1, source_target_pairs={{0,128},{16,144},{32,160},{48,176},{64,192},{80,208},{96,224},{112... | collective-permute-start | bytes 147464 | tf_op jit(solution)/shard_map/ppermute | solution.py:92
  25.1 11.7 %collective-permute-start.1 = (f32[32,384]{1,0:T(8,128)S(1)}, f32[32,384]{1,0:T(8,128)S(1)}, u32[]{:S(2)}, u32[]{:S(2)}) collective-permute-start(f32[32,384]{1,0:T(8,128)S(1)} %add.6), channel_id=1, source_target_pairs={{0,256},{16,272},{32,288},{48,304},{64,320},{80,336},{96,352},{112... | collective-permute-start | bytes 147464 | tf_op jit(solution)/shard_map/ppermute | solution.py:92
  37.6 51.7 %all-to-all-start.1 = ((f32[8,32,384]{2,1,0:T(8,128)}), f32[8,32,384]{2,1,0:T(8,128)S(1)}, u32[]{:S(2)}, u32[]{:S(2)}) async-start(f32[8,32,384]{2,1,0:T(8,128)} %broadcast_in_dim.3), calls=%async_computation.1 | async-start | bytes 786432 | tf_op jit(solution)/shard_map/all_to_all | solution.py:162
  48.6 3.3 %collective-permute-start.2 = (f32[8,8,256]{2,1,0:T(8,128)}, f32[8,8,256]{2,1,0:T(8,128)S(1)}, u32[]{:S(2)}, u32[]{:S(2)}) collective-permute-start(f32[8,8,256]{2,1,0:T(8,128)} %get-tuple-element.19), channel_id=1, source_target_pairs={{0,1},{1,0},{2,3},{3,2},{4,5},{5,4},{6,7},{7,6},{8,9},{9,8},{10,11... | collective-permute-start | bytes 196616 | tf_op jit(solution)/shard_map/ppermute | solution.py:92
  52.0 0.6 copy-start.1
  54.1 7.5 %collective-permute-start.3 = (f32[4,8,256]{2,1,0:T(8,128)}, f32[4,8,256]{2,1,0:T(8,128)S(1)}, u32[]{:S(2)}, u32[]{:S(2)}) collective-permute-start(f32[4,8,256]{2,1,0:T(8,128)} %get-tuple-element.21), channel_id=1, source_target_pairs={{0,8},{1,9},{2,10},{3,11},{4,12},{5,13},{6,14},{7,15},{8,0},{9,1},... | collective-permute-start | bytes 98312 | tf_op jit(solution)/shard_map/ppermute | solution.py:92
  61.6 0.6 copy-start.2
  63.6 5.8 %collective-permute-start.4 = (f32[2,8,256]{2,1,0:T(8,128)}, f32[2,8,256]{2,1,0:T(8,128)S(1)}, u32[]{:S(2)}, u32[]{:S(2)}) collective-permute-start(f32[2,8,256]{2,1,0:T(8,128)} %get-tuple-element.23), channel_id=1, source_target_pairs={{0,4},{1,5},{2,6},{3,7},{4,0},{5,1},{6,2},{7,3},{8,12},{9,13},{10,... | collective-permute-start | bytes 49160 | tf_op jit(solution)/shard_map/ppermute | solution.py:92
  69.4 0.6 copy-start.3
  71.3 16.1 %collective-permute-start.5 = (f32[1,8,256]{2,1,0:T(8,128)}, f32[1,8,256]{2,1,0:T(8,128)S(1)}, u32[]{:S(2)}, u32[]{:S(2)}) collective-permute-start(f32[1,8,256]{2,1,0:T(8,128)} %get-tuple-element.25), channel_id=1, source_target_pairs={{0,2},{1,3},{2,0},{3,1},{4,6},{5,7},{6,4},{7,5},{8,10},{9,11},{10,... | collective-permute-start | bytes 24584 | tf_op jit(solution)/shard_map/ppermute | solution.py:92
  87.4 0.6 copy-start.4
  89.3 0.7 copy-start

commit v2 on v1

v2 whole, which is shorter than its diff:
```python
import functools

import jax
import jax.numpy as jnp
from jax import lax
from jax.experimental import pallas as pl
from jax.experimental.pallas import tpu as pltpu
from jax.sharding import PartitionSpec as P

outer_rate = 0.7
outer_momentum = 0.9
slope_scale = 0.7978845608028654
carry = outer_momentum * outer_momentum / (1.0 + outer_momentum)
param_step = outer_rate * (1.0 + outer_momentum)
moment_rest = outer_momentum - carry
near = 8
block = 128
small = pltpu.CompilerParams(vmem_limit_bytes=4 << 20)


def full(shape):
    return pl.BlockSpec(shape, lambda *_: (0,) * len(shape))


def dequant_kernel(codes_ref, scales_ref, moment_ref, out_ref, *, groups):
    rows = codes_ref.shape[1]
    per_part = out_ref.shape[1] // rows
    own = lax.broadcasted_iota(jnp.int32, (rows, block), 0) == lax.axis_index("rep")
    scales = scales_ref[0].T * (1.0 / groups)
    for j in range(codes_ref.shape[2] // block):
        cols = slice(j * block, (j + 1) * block)
        grads = (codes_ref[0, :, cols].astype(jnp.float32) - 7.5) * scales[:, j : j + 1]
        kept = jnp.where(own, carry * moment_ref[:, cols], 0.0)
        part, k = divmod(j, per_part)
        out_ref[part, k * rows : (k + 1) * rows] = grads + kept


def backward_kernel(
    inputs_ref, pre_ref, grad_ref, weights_ref, wgrad_ref, send_ref, total
):
    step = pl.program_id(0)

    @pl.when(step == 0)
    def _():
        total[...] = jnp.zeros_like(total)

    v = pre_ref[...].astype(jnp.float32)
    u = v * v
    t = jnp.tanh(v * (slope_scale + (slope_scale * 0.044715) * u))
    slope = (0.5 + 0.5 * t) * (
        1.0 + (v * (slope_scale + (slope_scale * 0.134145) * u)) * (1.0 - t)
    )
    pre_grad = (grad_ref[...].astype(jnp.float32) * slope).astype(jnp.bfloat16)
    wgrad_ref[0] = lax.dot_general(
        inputs_ref[...], pre_grad, (((0,), (0,)), ((), ())), preferred_element_type=jnp.float32
    ).astype(jnp.bfloat16)
    total[...] += lax.dot_general(
        weights_ref[0], pre_grad, (((1,), (1,)), ((), ())), preferred_element_type=jnp.float32
    ).reshape(total.shape)

    @pl.when(step == pl.num_programs(0) - 1)
    def _():
        columns, sides = send_ref.shape[:2]
        for j in range(columns):
            for side in range(sides):
                send_ref[j, side] = total[(j // 2) * 4 + side * 2 + j % 2]


def pack_kernel(chunk_ref, moved_ref, came_ref, keep_ref, out_ref):
    size = chunk_ref.shape[0]
    side = (lax.axis_index("tp") // 2) % 2
    sums = []
    for at in (side, 1 - side):
        piece = came_ref[0, at]
        for j in range(1, came_ref.shape[0]):
            piece += came_ref[j, at]
        sums.append(piece)
    keep_ref[...] = sums[0]
    out_ref[:size] = chunk_ref[...] + moved_ref[...]
    height, width = sums[1].shape
    for k in range(width // block):
        out_ref[size + k * height : size + (k + 1) * height] = sums[1][:, k * block : (k + 1) * block]


def spread_kernel(mine_ref, came_ref, copies_ref, relay_ref):
    size = copies_ref.shape[1]
    copies_ref[...] = jnp.broadcast_to(mine_ref[:size] + came_ref[:size], copies_ref.shape)
    relay_ref[...] = came_ref[size:]


def join_kernel(kept_ref, came_ref, out_ref):
    height, width = out_ref.shape
    for k in range(width // block):
        cols = slice(k * block, (k + 1) * block)
        out_ref[:, cols] = (
            kept_ref[:, cols] + came_ref[k * height : (k + 1) * height]
        ).astype(out_ref.dtype)


def outer_kernel(sums_ref, params_ref, moment_ref, params_out_ref, moment_out_ref):
    rows = params_ref.shape[0]
    per_part = sums_ref.shape[1] // rows
    own = lax.axis_index("rep")
    for j in range(params_ref.shape[1] // block):
        cols = slice(j * block, (j + 1) * block)
        part, k = divmod(j, per_part)
        params_out_ref[:, cols] = (
            params_ref[:, cols] - param_step * sums_ref[part, k * rows : (k + 1) * rows]
        )
        moment_out_ref[:, cols] = (
            sums_ref[part, pl.ds(k * rows + own, 1), :] + moment_rest * moment_ref[:, cols]
        )


def swap(array, axis, bit):
    size = lax.axis_size(axis)
    return lax.ppermute(array, axis, [(i, i ^ bit) for i in range(size)])


def exchange(array, axis, groups):
    return lax.all_to_all(array, axis, 0, 0, axis_index_groups=groups, tiled=True)


def on_device(
    quant_codes, block_scales, outer_params, outer_moment, inputs, saved_pre, grad_out, weights
):
    groups = lax.axis_size("rep")
    _, rows, hidden = quant_codes.shape
    tokens, window = inputs.shape
    size = rows * hidden // (near * block)
    near_groups = [list(range(i, i + near)) for i in range(0, groups, near)]

    parts = pl.pallas_call(
        functools.partial(dequant_kernel, groups=groups),
        out_shape=jax.ShapeDtypeStruct((near, size, block), jnp.float32),
        name="dequant",
    )(quant_codes, jnp.transpose(block_scales, (0, 2, 1)), outer_moment)
    parts, inputs = lax.optimization_barrier((parts, inputs))
    parts = exchange(parts, "rep", near_groups)
    chunk = jnp.sum(parts, axis=0)

    tile = 512
    shares = lax.axis_size("tp")
    piece = (window // shares, tokens)
    sent = jax.ShapeDtypeStruct((shares // 2, 2) + piece, jnp.float32)
    weight_grad, send = pl.pallas_call(
        backward_kernel,
        grid=(hidden // tile,),
        in_specs=[
            full((tokens, window)),
            pl.BlockSpec((tokens, tile), lambda i: (0, i)),
            pl.BlockSpec((tokens, tile), lambda i: (0, i)),
            pl.BlockSpec((1, window, tile), lambda i: (0, 0, i)),
        ],
        out_specs=[
            pl.BlockSpec((1, window, tile), lambda i: (0, 0, i)),
            full(sent.shape),
        ],
        out_shape=(jax.ShapeDtypeStruct((1, window, hidden), jnp.bfloat16), sent),
        scratch_shapes=[pltpu.VMEM((shares,) + piece, jnp.float32)],
        cost_estimate=pl.CostEstimate(
            flops=4 * tokens * window * hidden,
            bytes_accessed=4 * tokens * hidden + 4 * window * hidden,
            transcendentals=tokens * hidden,
        ),
        compiler_params=pltpu.CompilerParams(vmem_limit_bytes=60 << 20),
        name="backward",
    )(inputs, saved_pre, grad_out, weights)

    chunk, send = lax.optimization_barrier((chunk, send))
    column_groups = [
        [i + side + core for i in range(0, shares, 4) for core in (0, 1)] for side in (0, 2)
    ]
    came = exchange(send, "tp", column_groups)
    moved = swap(chunk, "rep", near)
    extra = piece[0] * piece[1] // block
    keep, packed = pl.pallas_call(
        pack_kernel,
        out_shape=(
            jax.ShapeDtypeStruct(piece, jnp.float32),
            jax.ShapeDtypeStruct((size + extra, block), jnp.float32),
        ),
        compiler_params=small,
        name="pack",
    )(chunk, moved, came)
    came = swap(packed, "rep", 2 * near)
    copies, relay = pl.pallas_call(
        spread_kernel,
        out_shape=(
            jax.ShapeDtypeStruct((near, size, block), jnp.float32),
            jax.ShapeDtypeStruct((extra, block), jnp.float32),
        ),
        compiler_params=small,
        name="spread",
    )(packed, came)
    came = lax.ppermute(
        relay,
        ("rep", "tp"),
        [
            (i * shares + j, (i ^ (2 * near)) * shares + (j ^ 2))
            for i in range(groups)
            for j in range(shares)
        ],
    )
    input_grad_t = pl.pallas_call(
        join_kernel,
        out_shape=jax.ShapeDtypeStruct(piece, jnp.bfloat16),
        compiler_params=small,
        name="join",
    )(keep, came)
    sums = exchange(copies, "rep", near_groups)
    new_params, new_moment = pl.pallas_call(
        outer_kernel,
        out_shape=(
            jax.ShapeDtypeStruct(outer_params.shape, jnp.float32),
            jax.ShapeDtypeStruct(outer_moment.shape, jnp.float32),
        ),
        compiler_params=small, name="outer_step",
    )(sums, outer_params, outer_moment)
    return (new_params, new_moment, weight_grad, input_grad_t)


def solution(mesh):
    in_specs = (
        P("rep", None, "tp"),
        P("rep", None, "tp"),
        P(None, "tp"),
        P("rep", "tp"),
        P("rep", None),
        P("rep", "tp"),
        P("rep", "tp"),
        P("rep", None, "tp"),
    )
    out_specs = (P(None, "tp"), P("rep", "tp"), P("rep", None, "tp"), P("tp", "rep"))
    return jax.shard_map(
        on_device, mesh=mesh, in_specs=in_specs, out_specs=out_specs, check_vma=False
    )
```

time: 92.8 us -> 62.1 us (0.67)
  the two profiles are of different devices: /device:TPU:26 before, /device:TPU:66 now
where the time goes in v2:
time: 62.1 us; the launch traced here: 61.6 us
  starting transfers between devices  39.8 us (64%)
  Pallas kernels  10.7 us (17%)
  waiting for transfers between devices  10.4 us (17%)
  between operations  0.68 us (1%)
    all_to_all x3, starting transfers between devices, exchange(): lax.all_to_all(array, axis, 0, 0, axis_index_groups=groups, tiled=True)  17.6 us
    ppermute x2, starting transfers between devices, swap(): return lax.ppermute(array, axis, [(i, i ^ bit) for i in range(size)])  12.7 us
    ppermute x1, starting transfers between devices, on_device(): lax.ppermute(relay, ('rep', 'tp'), [(i * shares + j, (i ^ 2 * near) * sha...  9.54 us
    ppermute x2, waiting for transfers between devices, swap(): return lax.ppermute(array, axis, [(i, i ^ bit) for i in range(size)])  6.84 us
    pallas_call x1, Pallas kernels, on_device(): pl.pallas_call(backward_kernel, grid=(hidden // tile,), in_specs=[full((t...  6.43 us
    ppermute x1, waiting for transfers between devices, on_device(): lax.ppermute(relay, ('rep', 'tp'), [(i * shares + j, (i ^ 2 * near) * sha...  3.36 us
    pallas_call x1, Pallas kernels, on_device(): pl.pallas_call(functools.partial(dequant_kernel, groups=groups), out_shap...  2.06 us
  transfers between devices with their start and end apart: 6, of which 4 were waited for; matrix products, arithmetic and copies ran while one was open for 0% of the time, Pallas kernels for 11%

profile of v2, /device:TPU:66, one launch (start us, length us, event | category | flops | bytes accessed | tf_op | source)
XLA Modules:
  0.0 61.6 jit_solution(15408128802208302837)
XLA Ops:
  0.6 2.1 %dequant.1 = f32[8,96,128]{2,1,0:T(8,128)} custom-call(s32[1,32,3072]{2,1,0:T(8,128)} %codes_ref.1, f32[1,24,32]{2,1,0:T(8,128)} %bitcast.1, f32[1,3072]{1,0:T(1,128)} %moment_ref.3), custom_call_target="tpu_custom_call" | custom-call | tf_op jit(solution)/shard_map/dequant/pallas_call | solution.py:133
  2.7 6.2 %all-to-all-start = ((f32[8,96,128]{2,1,0:T(8,128)}), f32[8,96,128]{2,1,0:T(8,128)S(1)}, u32[]{:S(2)}, u32[]{:S(2)}) async-start(f32[8,96,128]{2,1,0:T(8,128)} %dequant.1), calls=%async_computation | async-start | bytes 786432 | tf_op jit(solution)/shard_map/all_to_all | solution.py:121
  8.9 6.4 %backward.1 = (bf16[1,128,3072]{2,1,0:T(8,128)(2,1)}, f32[8,2,8,256]{3,2,1,0:T(8,128)}) custom-call(bf16[256,128]{1,0:T(8,128)(2,1)} %inputs_ref, bf16[256,3072]{1,0:T(8,128)(2,1)} %pre_ref.1, bf16[256,3072]{1,0:T(8,128)(2,1)} %grad_ref.1, bf16[1,128,3072]{2,1,0:T(8,128)(2,1)} %weights_ref.1), custom_call_target="tpu_custom_call" | custom-call | flops 402653184 | bytes 4718592 | tf_op jit(solution)/shard_map/backward/pallas_call | solution.py:146
  15.3 0.0 copy-start
  15.3 0.0 copy-start.1
  15.3 0.2 all-to-all-done
  15.5 4.5 %all-to-all-start.1 = ((f32[8,2,8,256]{3,2,1,0:T(8,128)}), f32[8,2,8,256]{3,2,1,0:T(8,128)S(1)}, u32[]{:S(2)}, u32[]{:S(2)}) async-start(f32[8,2,8,256]{3,2,1,0:T(8,128)} %get-tuple-element.20), calls=%async_computation.1 | async-start | bytes 262144 | tf_op jit(solution)/shard_map/all_to_all | solution.py:121
  20.0 3.6 %collective-permute-start = (f32[96,128]{1,0:T(8,128)S(1)}, f32[96,128]{1,0:T(8,128)S(1)}, u32[]{:S(2)}, u32[]{:S(2)}) collective-permute-start(f32[96,128]{1,0:T(8,128)S(1)} %reduce_sum.9.chunk_ref), channel_id=1, source_target_pairs={{0,128},{16,144},{32,160},{48,176},{64,192},{80,208},{96,224},{112... | collective-permute-start | bytes 147464 | tf_op jit(solution)/shard_map/ppermute | solution.py:117
  23.6 3.5 %collective-permute-done.moved_ref = f32[96,128]{1,0:T(8,128)S(1)} collective-permute-done((f32[96,128]{1,0:T(8,128)S(1)}, f32[96,128]{1,0:T(8,128)S(1)}, u32[]{:S(2)}, u32[]{:S(2)}) %collective-permute-start) | collective-permute-done | bytes 49184 | tf_op jit(solution)/shard_map/ppermute | solution.py:117
  27.0 0.0 all-to-all-done.1.came_ref
  27.1 9.1 %collective-permute-start.1 = (f32[112,128]{1,0:T(8,128)S(1)}, f32[112,128]{1,0:T(8,128)S(1)}, u32[]{:S(2)}, u32[]{:S(2)}) collective-permute-start(f32[112,128]{1,0:T(8,128)S(1)} %get-tuple-element.21.mine_ref), channel_id=1, source_target_pairs={{0,256},{16,272},{32,288},{48,304},{64,320},{80,336},{96,352},{112... | collective-permute-start | bytes 172040 | tf_op jit(solution)/shard_map/ppermute | solution.py:117
  36.2 3.4 %collective-permute-done.1.came_ref = f32[112,128]{1,0:T(8,128)S(1)} collective-permute-done((f32[112,128]{1,0:T(8,128)S(1)}, f32[112,128]{1,0:T(8,128)S(1)}, u32[]{:S(2)}, u32[]{:S(2)}) %collective-permute-start.1) | collective-permute-done | bytes 57376 | tf_op jit(solution)/shard_map/ppermute | solution.py:117
  39.5 0.8 %spread.1 = (f32[8,96,128]{2,1,0:T(8,128)}, f32[16,128]{1,0:T(8,128)S(1)}) custom-call(f32[112,128]{1,0:T(8,128)S(1)} %get-tuple-element.21.mine_ref, f32[112,128]{1,0:T(8,128)S(1)} %collective-permute-done.1.came_ref), custom_call_target="tpu_custom_call" | custom-call | tf_op jit(solution)/shard_map/spread/pallas_call | solution.py:187
  40.3 6.9 %all-to-all-start.2 = ((f32[8,96,128]{2,1,0:T(8,128)}), f32[8,96,128]{2,1,0:T(8,128)S(1)}, u32[]{:S(2)}, u32[]{:S(2)}) async-start(f32[8,96,128]{2,1,0:T(8,128)} %get-tuple-element.22), calls=%async_computation.2 | async-start | bytes 786432 | tf_op jit(solution)/shard_map/all_to_all | solution.py:121
  47.2 9.5 %collective-permute-start.2 = (f32[16,128]{1,0:T(8,128)S(1)}, f32[16,128]{1,0:T(8,128)S(1)}, u32[]{:S(2)}, u32[]{:S(2)}) collective-permute-start(f32[16,128]{1,0:T(8,128)S(1)} %get-tuple-element.27), channel_id=1, source_target_pairs={{0,258},{1,259},{2,256},{3,257},{4,262},{5,263},{6,260},{7,261},{8... | collective-permute-start | bytes 24584 | tf_op jit(solution)/shard_map/ppermute | solution.py:196
  56.8 3.4 %collective-permute-done.2.came_ref = f32[16,128]{1,0:T(8,128)S(1)} collective-permute-done((f32[16,128]{1,0:T(8,128)S(1)}, f32[16,128]{1,0:T(8,128)S(1)}, u32[]{:S(2)}, u32[]{:S(2)}) %collective-permute-start.2) | collective-permute-done | bytes 8224 | tf_op jit(solution)/shard_map/ppermute | solution.py:196
  60.1 0.6 join.1
  60.7 0.0 all-to-all-done.2.sums_ref
  60.7 0.0 copy-done
  60.7 0.0 copy-done.1
  60.7 0.8 %outer_step.1 = (f32[32,3072]{1,0:T(8,128)}, f32[1,3072]{1,0:T(1,128)}) custom-call(f32[8,96,128]{2,1,0:T(8,128)S(1)} %all-to-all-done.2.sums_ref, f32[32,3072]{1,0:T(8,128)S(1)} %copy-done, f32[1,3072]{1,0:T(1,128)S(1)} %copy-done.1), custom_call_target="tpu_custom_call" | custom-call | tf_op jit(solution)/shard_map/outer_step/pallas_call | solution.py:212
  (2 shorter events, 0.1 us)
Async XLA Ops:
  2.7 12.8 %all-to-all-start = ((f32[8,96,128]{2,1,0:T(8,128)}), f32[8,96,128]{2,1,0:T(8,128)S(1)}, u32[]{:S(2)}, u32[]{:S(2)}) async-start(f32[8,96,128]{2,1,0:T(8,128)} %dequant.1), calls=%async_computation | async-start | bytes 786432 | tf_op jit(solution)/shard_map/all_to_all | solution.py:121
  15.3 45.4 %copy-start = (f32[32,3072]{1,0:T(8,128)S(1)}, f32[32,3072]{1,0:T(8,128)}, u32[]{:S(2)}) copy-start(f32[32,3072]{1,0:T(8,128)} %params_ref.1) | copy-start | bytes 1179652
  15.3 45.4 %copy-start.1 = (f32[1,3072]{1,0:T(1,128)S(1)}, f32[1,3072]{1,0:T(1,128)}, u32[]{:S(2)}) copy-start(f32[1,3072]{1,0:T(1,128)} %moment_ref.3) | copy-start | bytes 36868
  15.5 11.5 %all-to-all-start.1 = ((f32[8,2,8,256]{3,2,1,0:T(8,128)}), f32[8,2,8,256]{3,2,1,0:T(8,128)S(1)}, u32[]{:S(2)}, u32[]{:S(2)}) async-start(f32[8,2,8,256]{3,2,1,0:T(8,128)} %get-tuple-element.20), calls=%async_computation.1 | async-start | bytes 262144 | tf_op jit(solution)/shard_map/all_to_all | solution.py:121
  20.0 7.0 %collective-permute-start = (f32[96,128]{1,0:T(8,128)S(1)}, f32[96,128]{1,0:T(8,128)S(1)}, u32[]{:S(2)}, u32[]{:S(2)}) collective-permute-start(f32[96,128]{1,0:T(8,128)S(1)} %reduce_sum.9.chunk_ref), channel_id=1, source_target_pairs={{0,128},{16,144},{32,160},{48,176},{64,192},{80,208},{96,224},{112... | collective-permute-start | bytes 147464 | tf_op jit(solution)/shard_map/ppermute | solution.py:117
  27.1 12.5 %collective-permute-start.1 = (f32[112,128]{1,0:T(8,128)S(1)}, f32[112,128]{1,0:T(8,128)S(1)}, u32[]{:S(2)}, u32[]{:S(2)}) collective-permute-start(f32[112,128]{1,0:T(8,128)S(1)} %get-tuple-element.21.mine_ref), channel_id=1, source_target_pairs={{0,256},{16,272},{32,288},{48,304},{64,320},{80,336},{96,352},{112... | collective-permute-start | bytes 172040 | tf_op jit(solution)/shard_map/ppermute | solution.py:117
  40.3 20.4 %all-to-all-start.2 = ((f32[8,96,128]{2,1,0:T(8,128)}), f32[8,96,128]{2,1,0:T(8,128)S(1)}, u32[]{:S(2)}, u32[]{:S(2)}) async-start(f32[8,96,128]{2,1,0:T(8,128)} %get-tuple-element.22), calls=%async_computation.2 | async-start | bytes 786432 | tf_op jit(solution)/shard_map/all_to_all | solution.py:121
  47.2 12.9 %collective-permute-start.2 = (f32[16,128]{1,0:T(8,128)S(1)}, f32[16,128]{1,0:T(8,128)S(1)}, u32[]{:S(2)}, u32[]{:S(2)}) collective-permute-start(f32[16,128]{1,0:T(8,128)S(1)} %get-tuple-element.27), channel_id=1, source_target_pairs={{0,258},{1,259},{2,256},{3,257},{4,262},{5,263},{6,260},{7,261},{8... | collective-permute-start | bytes 24584 | tf_op jit(solution)/shard_map/ppermute | solution.py:196

commit v3 on v2

--- a/solution.py
+++ b/solution.py
@@ -66,38 +66,37 @@
                 send_ref[j, side] = total[(j // 2) * 4 + side * 2 + j % 2]
 
 
-def pack_kernel(chunk_ref, moved_ref, came_ref, keep_ref, out_ref):
-    size = chunk_ref.shape[0]
+def side_kernel(came_ref, keep_ref, send_ref):
     side = (lax.axis_index("tp") // 2) % 2
-    sums = []
-    for at in (side, 1 - side):
+    for out_ref, at in ((keep_ref, side), (send_ref, 1 - side)):
         piece = came_ref[0, at]
         for j in range(1, came_ref.shape[0]):
             piece += came_ref[j, at]
-        sums.append(piece)
-    keep_ref[...] = sums[0]
-    out_ref[:size] = chunk_ref[...] + moved_ref[...]
-    height, width = sums[1].shape
-    for k in range(width // block):
-        out_ref[size + k * height : size + (k + 1) * height] = sums[1][:, k * block : (k + 1) * block]
-
-
-def spread_kernel(mine_ref, came_ref, copies_ref, relay_ref):
-    size = copies_ref.shape[1]
-    copies_ref[...] = jnp.broadcast_to(mine_ref[:size] + came_ref[:size], copies_ref.shape)
-    relay_ref[...] = came_ref[size:]
-
-
-def join_kernel(kept_ref, came_ref, out_ref):
-    height, width = out_ref.shape
-    for k in range(width // block):
-        cols = slice(k * block, (k + 1) * block)
-        out_ref[:, cols] = (
-            kept_ref[:, cols] + came_ref[k * height : (k + 1) * height]
-        ).astype(out_ref.dtype)
-
-
-def outer_kernel(sums_ref, params_ref, moment_ref, params_out_ref, moment_out_ref):
+        out_ref[...] = piece
+
+
+def add_kernel(mine_ref, came_ref, out_ref):
+    out_ref[...] = mine_ref[...] + came_ref[...]
+
+
+def relay_kernel(came_ref, out_ref):
+    out_ref[...] = came_ref[...]
+
+
+def spread_kernel(mine_ref, came_ref, copies_ref):
+    copies_ref[...] = jnp.broadcast_to(mine_ref[...] + came_ref[...], copies_ref.shape)
+
+
+def finish_kernel(
+    sums_ref,
+    params_ref,
+    moment_ref,
+    kept_ref,
+    came_ref,
+    params_out_ref,
+    moment_out_ref,
+    igrad_out_ref,
+):
     rows = params_ref.shape[0]
     per_part = sums_ref.shape[1] // rows
     own = lax.axis_index("rep")
@@ -110,6 +109,7 @@
         moment_out_ref[:, cols] = (
             sums_ref[part, pl.ds(k * rows + own, 1), :] + moment_rest * moment_ref[:, cols]
         )
+    igrad_out_ref[...] = (kept_ref[...] + came_ref[...]).astype(igrad_out_ref.dtype)
 
 
 def swap(array, axis, bit):
@@ -167,34 +167,17 @@
         name="backward",
     )(inputs, saved_pre, grad_out, weights)
 
-    chunk, send = lax.optimization_barrier((chunk, send))
+    chunk, _ = lax.optimization_barrier((chunk, send))
     column_groups = [
         [i + side + core for i in range(0, shares, 4) for core in (0, 1)] for side in (0, 2)
     ]
     came = exchange(send, "tp", column_groups)
-    moved = swap(chunk, "rep", near)
-    extra = piece[0] * piece[1] // block
-    keep, packed = pl.pallas_call(
-        pack_kernel,
-        out_shape=(
-            jax.ShapeDtypeStruct(piece, jnp.float32),
-            jax.ShapeDtypeStruct((size + extra, block), jnp.float32),
-        ),
-        compiler_params=small,
-        name="pack",
-    )(chunk, moved, came)
-    came = swap(packed, "rep", 2 * near)
-    copies, relay = pl.pallas_call(
-        spread_kernel,
-        out_shape=(
-            jax.ShapeDtypeStruct((near, size, block), jnp.float32),
-            jax.ShapeDtypeStruct((extra, block), jnp.float32),
-        ),
-        compiler_params=small,
-        name="spread",
-    )(packed, came)
+    part = jax.ShapeDtypeStruct(piece, jnp.float32)
+    keep, send = pl.pallas_call(
+        side_kernel, out_shape=(part, part), compiler_params=small, name="column_sum"
+    )(came)
     came = lax.ppermute(
-        relay,
+        send,
         ("rep", "tp"),
         [
             (i * shares + j, (i ^ (2 * near)) * shares + (j ^ 2))
@@ -202,21 +185,40 @@
             for j in range(shares)
         ],
     )
-    input_grad_t = pl.pallas_call(
-        join_kernel,
-        out_shape=jax.ShapeDtypeStruct(piece, jnp.bfloat16),
-        compiler_params=small,
-        name="join",
-    )(keep, came)
+    moved = swap(chunk, "rep", near)
+    chunk = pl.pallas_call(
+        add_kernel,
+        out_shape=jax.ShapeDtypeStruct(chunk.shape, jnp.float32),
+        compiler_params=small,
+        cost_estimate=pl.CostEstimate(flops=10**11, bytes_accessed=10**9, transcendentals=0),
+        name="pair_sum",
+    )(chunk, moved)
+    moved = swap(chunk, "rep", 2 * near)
+    copies = pl.pallas_call(
+        spread_kernel,
+        out_shape=jax.ShapeDtypeStruct((near, size, block), jnp.float32),
+        compiler_params=small,
+        name="spread",
+    )(chunk, moved)
+    came = pl.pallas_call(
+        relay_kernel,
+        out_shape=part,
+        compiler_params=small,
+        cost_estimate=pl.CostEstimate(flops=10**11, bytes_accessed=10**9, transcendentals=0),
+        name="relay",
+    )(came)
+    came = swap(came, "rep", 2 * near)
     sums = exchange(copies, "rep", near_groups)
-    new_params, new_moment = pl.pallas_call(
-        outer_kernel,
+    new_params, new_moment, input_grad_t = pl.pallas_call(
+        finish_kernel,
         out_shape=(
             jax.ShapeDtypeStruct(outer_params.shape, jnp.float32),
             jax.ShapeDtypeStruct(outer_moment.shape, jnp.float32),
+            jax.ShapeDtypeStruct(piece, jnp.bfloat16),
         ),
-        compiler_params=small, name="outer_step",
-    )(sums, outer_params, outer_moment)
+        compiler_params=small,
+        name="finish",
+    )(sums, outer_params, outer_moment, keep, came)
     return (new_params, new_moment, weight_grad, input_grad_t)
 
 

time: 62.1 us -> 58.8 us (0.947)
  the two profiles are of different devices: /device:TPU:66 before, /device:TPU:2 now
where the time goes in v3:
time: 58.8 us; the launch traced here: 58.1 us
  starting transfers between devices  43.1 us (73%)
  Pallas kernels  10.1 us (17%)
  waiting for transfers between devices  4.12 us (7%)
  between operations  0.72 us (1%)
    all_to_all x3, starting transfers between devices, exchange(): lax.all_to_all(array, axis, 0, 0, axis_index_groups=groups, tiled=True)  19.3 us
    ppermute x3, starting transfers between devices, swap(): return lax.ppermute(array, axis, [(i, i ^ bit) for i in range(size)])  16.8 us
    ppermute x1, starting transfers between devices, on_device(): lax.ppermute(send, ('rep', 'tp'), [(i * shares + j, (i ^ 2 * near) * shar...  7.01 us
    pallas_call x1, Pallas kernels, on_device(): pl.pallas_call(backward_kernel, grid=(hidden // tile,), in_specs=[full((t...  6.43 us
    ppermute x3, waiting for transfers between devices, swap(): return lax.ppermute(array, axis, [(i, i ^ bit) for i in range(size)])  4.11 us
    pallas_call x1, Pallas kernels, on_device(): pl.pallas_call(functools.partial(dequant_kernel, groups=groups), out_shap...  2.06 us
  transfers between devices with their start and end apart: 7, of which 2 were waited for; matrix products, arithmetic and copies ran while one was open for 0% of the time, Pallas kernels for 12%

profile of v3, /device:TPU:2, one launch (start us, length us, event | category | flops | bytes accessed | tf_op | source)
XLA Modules:
  0.0 58.1 jit_solution(3601476259843164508)
XLA Ops:
  0.6 2.1 %dequant.1 = f32[8,96,128]{2,1,0:T(8,128)} custom-call(s32[1,32,3072]{2,1,0:T(8,128)} %codes_ref.1, f32[1,24,32]{2,1,0:T(8,128)} %bitcast.1, f32[1,3072]{1,0:T(1,128)} %moment_ref.3), custom_call_target="tpu_custom_call" | custom-call | tf_op jit(solution)/shard_map/dequant/pallas_call | solution.py:133
  2.7 9.3 %all-to-all-start = ((f32[8,96,128]{2,1,0:T(8,128)}), f32[8,96,128]{2,1,0:T(8,128)S(1)}, u32[]{:S(2)}, u32[]{:S(2)}) async-start(f32[8,96,128]{2,1,0:T(8,128)} %dequant.1), calls=%async_computation | async-start | bytes 786432 | tf_op jit(solution)/shard_map/all_to_all | solution.py:121
  11.9 6.4 %backward.1 = (bf16[1,128,3072]{2,1,0:T(8,128)(2,1)}, f32[8,2,8,256]{3,2,1,0:T(8,128)}) custom-call(bf16[256,128]{1,0:T(8,128)(2,1)} %inputs_ref, bf16[256,3072]{1,0:T(8,128)(2,1)} %pre_ref.1, bf16[256,3072]{1,0:T(8,128)(2,1)} %grad_ref.1, bf16[1,128,3072]{2,1,0:T(8,128)(2,1)} %weights_ref.1), custom_call_target="tpu_custom_call" | custom-call | flops 402653184 | bytes 4718592 | tf_op jit(solution)/shard_map/backward/pallas_call | solution.py:146
  18.4 0.0 all-to-all-done
  18.4 2.3 %collective-permute-start = (f32[96,128]{1,0:T(8,128)S(1)}, f32[96,128]{1,0:T(8,128)S(1)}, u32[]{:S(2)}, u32[]{:S(2)}) collective-permute-start(f32[96,128]{1,0:T(8,128)S(1)} %reduce_sum.9.mine_ref), channel_id=1, source_target_pairs={{0,128},{16,144},{32,160},{48,176},{64,192},{80,208},{96,224},{112... | collective-permute-start | bytes 147464 | tf_op jit(solution)/shard_map/ppermute | solution.py:117
  20.7 4.5 %all-to-all-start.2 = ((f32[8,2,8,256]{3,2,1,0:T(8,128)}), f32[8,2,8,256]{3,2,1,0:T(8,128)S(1)}, u32[]{:S(2)}, u32[]{:S(2)}) async-start(f32[8,2,8,256]{3,2,1,0:T(8,128)} %get-tuple-element.16), calls=%async_computation.2 | async-start | bytes 262144 | tf_op jit(solution)/shard_map/all_to_all | solution.py:121
  25.2 0.1 collective-permute-done.came_ref
  25.3 9.0 %collective-permute-start.1 = (f32[96,128]{1,0:T(8,128)S(1)}, f32[96,128]{1,0:T(8,128)S(1)}, u32[]{:S(2)}, u32[]{:S(2)}) collective-permute-start(f32[96,128]{1,0:T(8,128)S(1)} %pair_sum.1.mine_ref), channel_id=1, source_target_pairs={{0,256},{16,272},{32,288},{48,304},{64,320},{80,336},{96,352},{112... | collective-permute-start | bytes 147464 | tf_op jit(solution)/shard_map/ppermute | solution.py:117
  34.3 0.0 all-to-all-done.2.came_ref
  34.4 7.0 %collective-permute-start.2 = (f32[8,256]{1,0:T(8,128)S(1)}, f32[8,256]{1,0:T(8,128)S(1)}, u32[]{:S(2)}, u32[]{:S(2)}) collective-permute-start(f32[8,256]{1,0:T(8,128)S(1)} %get-tuple-element.19), channel_id=1, source_target_pairs={{0,258},{1,259},{2,256},{3,257},{4,262},{5,263},{6,260},{7,261},{8... | collective-permute-start | bytes 24584 | tf_op jit(solution)/shard_map/ppermute | solution.py:179
  41.4 0.0 collective-permute-done.1.came_ref
  41.4 0.8 %spread.1 = f32[8,96,128]{2,1,0:T(8,128)} custom-call(f32[96,128]{1,0:T(8,128)S(1)} %pair_sum.1.mine_ref, f32[96,128]{1,0:T(8,128)S(1)} %collective-permute-done.1.came_ref), custom_call_target="tpu_custom_call" | custom-call | tf_op jit(solution)/shard_map/spread/pallas_call | solution.py:197
  42.2 5.5 %all-to-all-start.1 = ((f32[8,96,128]{2,1,0:T(8,128)}), f32[8,96,128]{2,1,0:T(8,128)S(1)}, u32[]{:S(2)}, u32[]{:S(2)}) async-start(f32[8,96,128]{2,1,0:T(8,128)} %spread.1), calls=%async_computation.1 | async-start | bytes 786432 | tf_op jit(solution)/shard_map/all_to_all | solution.py:121
  47.7 0.0 copy-start
  47.7 0.0 copy-start.1
  47.7 0.0 collective-permute-done.2.came_ref
  47.7 5.6 %collective-permute-start.3 = (f32[8,256]{1,0:T(8,128)S(1)}, f32[8,256]{1,0:T(8,128)S(1)}, u32[]{:S(2)}, u32[]{:S(2)}) collective-permute-start(f32[8,256]{1,0:T(8,128)S(1)} %relay.1), channel_id=1, source_target_pairs={{0,256},{16,272},{32,288},{48,304},{64,320},{80,336},{96,352},{112... | collective-permute-start | bytes 24584 | tf_op jit(solution)/shard_map/ppermute | solution.py:117
  53.3 4.0 %collective-permute-done.3.came_ref = f32[8,256]{1,0:T(8,128)S(1)} collective-permute-done((f32[8,256]{1,0:T(8,128)S(1)}, f32[8,256]{1,0:T(8,128)S(1)}, u32[]{:S(2)}, u32[]{:S(2)}) %collective-permute-start.3) | collective-permute-done | bytes 8224 | tf_op jit(solution)/shard_map/ppermute | solution.py:117
  57.3 0.0 all-to-all-done.1.sums_ref
  57.3 0.0 copy-done
  57.3 0.0 copy-done.1
  57.3 0.8 %finish.1 = (f32[32,3072]{1,0:T(8,128)}, f32[1,3072]{1,0:T(1,128)}, bf16[8,256]{1,0:T(8,128)(2,1)}) custom-call(f32[8,96,128]{2,1,0:T(8,128)S(1)} %all-to-all-done.1.sums_ref, f32[32,3072]{1,0:T(8,128)S(1)} %copy-done, f32[1,3072]{1,0:T(1,128)S(1)} %copy-done.1, f32[8,256]{1,0:T(8,128)S(1)} %get-tuple-element.18.kept_ref, ...), custom_call_target="tpu_custom_call" | custom-call | tf_op jit(solution)/shard_map/finish/pallas_call | solution.py:212
  (4 shorter events, 0.1 us)
Async XLA Ops:
  2.7 15.7 %all-to-all-start = ((f32[8,96,128]{2,1,0:T(8,128)}), f32[8,96,128]{2,1,0:T(8,128)S(1)}, u32[]{:S(2)}, u32[]{:S(2)}) async-start(f32[8,96,128]{2,1,0:T(8,128)} %dequant.1), calls=%async_computation | async-start | bytes 786432 | tf_op jit(solution)/shard_map/all_to_all | solution.py:121
  18.4 6.9 %collective-permute-start = (f32[96,128]{1,0:T(8,128)S(1)}, f32[96,128]{1,0:T(8,128)S(1)}, u32[]{:S(2)}, u32[]{:S(2)}) collective-permute-start(f32[96,128]{1,0:T(8,128)S(1)} %reduce_sum.9.mine_ref), channel_id=1, source_target_pairs={{0,128},{16,144},{32,160},{48,176},{64,192},{80,208},{96,224},{112... | collective-permute-start | bytes 147464 | tf_op jit(solution)/shard_map/ppermute | solution.py:117
  20.7 13.6 %all-to-all-start.2 = ((f32[8,2,8,256]{3,2,1,0:T(8,128)}), f32[8,2,8,256]{3,2,1,0:T(8,128)S(1)}, u32[]{:S(2)}, u32[]{:S(2)}) async-start(f32[8,2,8,256]{3,2,1,0:T(8,128)} %get-tuple-element.16), calls=%async_computation.2 | async-start | bytes 262144 | tf_op jit(solution)/shard_map/all_to_all | solution.py:121
  25.3 16.1 %collective-permute-start.1 = (f32[96,128]{1,0:T(8,128)S(1)}, f32[96,128]{1,0:T(8,128)S(1)}, u32[]{:S(2)}, u32[]{:S(2)}) collective-permute-start(f32[96,128]{1,0:T(8,128)S(1)} %pair_sum.1.mine_ref), channel_id=1, source_target_pairs={{0,256},{16,272},{32,288},{48,304},{64,320},{80,336},{96,352},{112... | collective-permute-start | bytes 147464 | tf_op jit(solution)/shard_map/ppermute | solution.py:117
  34.4 13.3 %collective-permute-start.2 = (f32[8,256]{1,0:T(8,128)S(1)}, f32[8,256]{1,0:T(8,128)S(1)}, u32[]{:S(2)}, u32[]{:S(2)}) collective-permute-start(f32[8,256]{1,0:T(8,128)S(1)} %get-tuple-element.19), channel_id=1, source_target_pairs={{0,258},{1,259},{2,256},{3,257},{4,262},{5,263},{6,260},{7,261},{8... | collective-permute-start | bytes 24584 | tf_op jit(solution)/shard_map/ppermute | solution.py:179
  42.2 15.1 %all-to-all-start.1 = ((f32[8,96,128]{2,1,0:T(8,128)}), f32[8,96,128]{2,1,0:T(8,128)S(1)}, u32[]{:S(2)}, u32[]{:S(2)}) async-start(f32[8,96,128]{2,1,0:T(8,128)} %spread.1), calls=%async_computation.1 | async-start | bytes 786432 | tf_op jit(solution)/shard_map/all_to_all | solution.py:121
  47.7 9.6 %copy-start = (f32[32,3072]{1,0:T(8,128)S(1)}, f32[32,3072]{1,0:T(8,128)}, u32[]{:S(2)}) copy-start(f32[32,3072]{1,0:T(8,128)} %params_ref.1) | copy-start | bytes 1179652
  47.7 9.6 %copy-start.1 = (f32[1,3072]{1,0:T(1,128)S(1)}, f32[1,3072]{1,0:T(1,128)}, u32[]{:S(2)}) copy-start(f32[1,3072]{1,0:T(1,128)} %moment_ref.3) | copy-start | bytes 36868
  47.7 9.6 %collective-permute-start.3 = (f32[8,256]{1,0:T(8,128)S(1)}, f32[8,256]{1,0:T(8,128)S(1)}, u32[]{:S(2)}, u32[]{:S(2)}) collective-permute-start(f32[8,256]{1,0:T(8,128)S(1)} %relay.1), channel_id=1, source_target_pairs={{0,256},{16,272},{32,288},{48,304},{64,320},{80,336},{96,352},{112... | collective-permute-start | bytes 24584 | tf_op jit(solution)/shard_map/ppermute | solution.py:117

commit v4 on v3

--- a/solution.py
+++ b/solution.py
@@ -139,7 +139,7 @@
     parts = exchange(parts, "rep", near_groups)
     chunk = jnp.sum(parts, axis=0)
 
-    tile = 512
+    tile = 1536
     shares = lax.axis_size("tp")
     piece = (window // shares, tokens)
     sent = jax.ShapeDtypeStruct((shares // 2, 2) + piece, jnp.float32)
@@ -180,7 +180,7 @@
         send,
         ("rep", "tp"),
         [
-            (i * shares + j, (i ^ (2 * near)) * shares + (j ^ 2))
+            (i * shares + j, (i ^ near) * shares + (j ^ 2))
             for i in range(groups)
             for j in range(shares)
         ],
@@ -207,7 +207,7 @@
         cost_estimate=pl.CostEstimate(flops=10**11, bytes_accessed=10**9, transcendentals=0),
         name="relay",
     )(came)
-    came = swap(came, "rep", 2 * near)
+    came = swap(came, "rep", near)
     sums = exchange(copies, "rep", near_groups)
     new_params, new_moment, input_grad_t = pl.pallas_call(
         finish_kernel,

time: 58.8 us -> 57.6 us (0.980)
  the two profiles are of different devices: /device:TPU:2 before, /device:TPU:8 now
where the time goes in v4:
time: 57.6 us; the launch traced here: 57 us
  starting transfers between devices  38.9 us (68%)
  Pallas kernels  8.92 us (15%)
  waiting for transfers between devices  8.42 us (15%)
  between operations  0.72 us (1%)
    ppermute x3, starting transfers between devices, swap(): return lax.ppermute(array, axis, [(i, i ^ bit) for i in range(size)])  17.3 us
    all_to_all x3, starting transfers between devices, exchange(): lax.all_to_all(array, axis, 0, 0, axis_index_groups=groups, tiled=True)  14 us
    ppermute x1, starting transfers between devices, on_device(): lax.ppermute(send, ('rep', 'tp'), [(i * shares + j, (i ^ near) * shares +...  7.64 us
    pallas_call x1, Pallas kernels, on_device(): pl.pallas_call(backward_kernel, grid=(hidden // tile,), in_specs=[full((t...  5.21 us
    all_to_all x3, waiting for transfers between devices, exchange(): lax.all_to_all(array, axis, 0, 0, axis_index_groups=groups, tiled=True)  4.45 us
    ppermute x3, waiting for transfers between devices, swap(): return lax.ppermute(array, axis, [(i, i ^ bit) for i in range(size)])  3.43 us
    pallas_call x1, Pallas kernels, on_device(): pl.pallas_call(functools.partial(dequant_kernel, groups=groups), out_shap...  2.06 us
  transfers between devices with their start and end apart: 7, of which 4 were waited for; matrix products, arithmetic and copies ran while one was open for 0% of the time, Pallas kernels for 11%

profile of v4, /device:TPU:8, one launch (start us, length us, event | category | flops | bytes accessed | tf_op | source)
XLA Modules:
  0.0 57.0 jit_solution(8631376058259171014)
XLA Ops:
  0.6 2.1 %dequant.1 = f32[8,96,128]{2,1,0:T(8,128)} custom-call(s32[1,32,3072]{2,1,0:T(8,128)} %codes_ref.1, f32[1,24,32]{2,1,0:T(8,128)} %bitcast.1, f32[1,3072]{1,0:T(1,128)} %moment_ref.3), custom_call_target="tpu_custom_call" | custom-call | tf_op jit(solution)/shard_map/dequant/pallas_call | solution.py:133
  2.7 5.7 %all-to-all-start = ((f32[8,96,128]{2,1,0:T(8,128)}), f32[8,96,128]{2,1,0:T(8,128)S(1)}, u32[]{:S(2)}, u32[]{:S(2)}) async-start(f32[8,96,128]{2,1,0:T(8,128)} %dequant.1), calls=%async_computation | async-start | bytes 786432 | tf_op jit(solution)/shard_map/all_to_all | solution.py:121
  8.3 5.2 %backward.1 = (bf16[1,128,3072]{2,1,0:T(8,128)(2,1)}, f32[8,2,8,256]{3,2,1,0:T(8,128)}) custom-call(bf16[256,128]{1,0:T(8,128)(2,1)} %inputs_ref, bf16[256,3072]{1,0:T(8,128)(2,1)} %pre_ref.1, bf16[256,3072]{1,0:T(8,128)(2,1)} %grad_ref.1, bf16[1,128,3072]{2,1,0:T(8,128)(2,1)} %weights_ref.1), custom_call_target="tpu_custom_call" | custom-call | flops 402653184 | bytes 4718592 | tf_op jit(solution)/shard_map/backward/pallas_call | solution.py:146
  13.6 3.2 %all-to-all-done = f32[8,96,128]{2,1,0:T(8,128)S(1)} async-done(((f32[8,96,128]{2,1,0:T(8,128)}), f32[8,96,128]{2,1,0:T(8,128)S(1)}, u32[]{:S(2)}, u32[]{:S(2)}) %all-to-all-start) | async-done | bytes 393248 | tf_op jit(solution)/shard_map/all_to_all | solution.py:121
  16.8 5.2 %collective-permute-start = (f32[96,128]{1,0:T(8,128)S(1)}, f32[96,128]{1,0:T(8,128)S(1)}, u32[]{:S(2)}, u32[]{:S(2)}) collective-permute-start(f32[96,128]{1,0:T(8,128)S(1)} %reduce_sum.9.mine_ref), channel_id=1, source_target_pairs={{0,128},{16,144},{32,160},{48,176},{64,192},{80,208},{96,224},{112... | collective-permute-start | bytes 147464 | tf_op jit(solution)/shard_map/ppermute | solution.py:117
  22.0 4.9 %all-to-all-start.2 = ((f32[8,2,8,256]{3,2,1,0:T(8,128)}), f32[8,2,8,256]{3,2,1,0:T(8,128)S(1)}, u32[]{:S(2)}, u32[]{:S(2)}) async-start(f32[8,2,8,256]{3,2,1,0:T(8,128)} %get-tuple-element.16), calls=%async_computation.2 | async-start | bytes 262144 | tf_op jit(solution)/shard_map/all_to_all | solution.py:121
  26.9 0.0 collective-permute-done.came_ref
  27.0 9.1 %collective-permute-start.1 = (f32[96,128]{1,0:T(8,128)S(1)}, f32[96,128]{1,0:T(8,128)S(1)}, u32[]{:S(2)}, u32[]{:S(2)}) collective-permute-start(f32[96,128]{1,0:T(8,128)S(1)} %pair_sum.1.mine_ref), channel_id=1, source_target_pairs={{0,256},{16,272},{32,288},{48,304},{64,320},{80,336},{96,352},{112... | collective-permute-start | bytes 147464 | tf_op jit(solution)/shard_map/ppermute | solution.py:117
  36.1 0.0 all-to-all-done.2.came_ref
  36.1 7.6 %collective-permute-start.2 = (f32[8,256]{1,0:T(8,128)S(1)}, f32[8,256]{1,0:T(8,128)S(1)}, u32[]{:S(2)}, u32[]{:S(2)}) collective-permute-start(f32[8,256]{1,0:T(8,128)S(1)} %get-tuple-element.19), channel_id=1, source_target_pairs={{0,130},{1,131},{2,128},{3,129},{4,134},{5,135},{6,132},{7,133},{8... | collective-permute-start | bytes 24584 | tf_op jit(solution)/shard_map/ppermute | solution.py:179
  43.8 0.0 collective-permute-done.1.came_ref
  43.8 0.8 %spread.1 = f32[8,96,128]{2,1,0:T(8,128)} custom-call(f32[96,128]{1,0:T(8,128)S(1)} %pair_sum.1.mine_ref, f32[96,128]{1,0:T(8,128)S(1)} %collective-permute-done.1.came_ref), custom_call_target="tpu_custom_call" | custom-call | tf_op jit(solution)/shard_map/spread/pallas_call | solution.py:197
  44.6 3.5 %all-to-all-start.1 = ((f32[8,96,128]{2,1,0:T(8,128)}), f32[8,96,128]{2,1,0:T(8,128)S(1)}, u32[]{:S(2)}, u32[]{:S(2)}) async-start(f32[8,96,128]{2,1,0:T(8,128)} %spread.1), calls=%async_computation.1 | async-start | bytes 786432 | tf_op jit(solution)/shard_map/all_to_all | solution.py:121
  48.0 0.0 copy-start
  48.0 0.0 copy-start.1
  48.0 0.5 collective-permute-done.2.came_ref
  48.6 3.0 %collective-permute-start.3 = (f32[8,256]{1,0:T(8,128)S(1)}, f32[8,256]{1,0:T(8,128)S(1)}, u32[]{:S(2)}, u32[]{:S(2)}) collective-permute-start(f32[8,256]{1,0:T(8,128)S(1)} %relay.1), channel_id=1, source_target_pairs={{0,128},{16,144},{32,160},{48,176},{64,192},{80,208},{96,224},{112... | collective-permute-start | bytes 24584 | tf_op jit(solution)/shard_map/ppermute | solution.py:117
  51.6 3.4 %collective-permute-done.3.came_ref = f32[8,256]{1,0:T(8,128)S(1)} collective-permute-done((f32[8,256]{1,0:T(8,128)S(1)}, f32[8,256]{1,0:T(8,128)S(1)}, u32[]{:S(2)}, u32[]{:S(2)}) %collective-permute-start.3) | collective-permute-done | bytes 8224 | tf_op jit(solution)/shard_map/ppermute | solution.py:117
  55.0 1.2 %all-to-all-done.1.sums_ref = f32[8,96,128]{2,1,0:T(8,128)S(1)} async-done(((f32[8,96,128]{2,1,0:T(8,128)}), f32[8,96,128]{2,1,0:T(8,128)S(1)}, u32[]{:S(2)}, u32[]{:S(2)}) %all-to-all-start.1) | async-done | bytes 393248 | tf_op jit(solution)/shard_map/all_to_all | solution.py:121
  56.2 0.0 copy-done
  56.2 0.0 copy-done.1
  56.2 0.8 %finish.1 = (f32[32,3072]{1,0:T(8,128)}, f32[1,3072]{1,0:T(1,128)}, bf16[8,256]{1,0:T(8,128)(2,1)}) custom-call(f32[8,96,128]{2,1,0:T(8,128)S(1)} %all-to-all-done.1.sums_ref, f32[32,3072]{1,0:T(8,128)S(1)} %copy-done, f32[1,3072]{1,0:T(1,128)S(1)} %copy-done.1, f32[8,256]{1,0:T(8,128)S(1)} %get-tuple-element.18.kept_ref, ...), custom_call_target="tpu_custom_call" | custom-call | tf_op jit(solution)/shard_map/finish/pallas_call | solution.py:212
  (4 shorter events, 0.1 us)
Async XLA Ops:
  2.7 14.1 %all-to-all-start = ((f32[8,96,128]{2,1,0:T(8,128)}), f32[8,96,128]{2,1,0:T(8,128)S(1)}, u32[]{:S(2)}, u32[]{:S(2)}) async-start(f32[8,96,128]{2,1,0:T(8,128)} %dequant.1), calls=%async_computation | async-start | bytes 786432 | tf_op jit(solution)/shard_map/all_to_all | solution.py:121
  16.8 10.1 %collective-permute-start = (f32[96,128]{1,0:T(8,128)S(1)}, f32[96,128]{1,0:T(8,128)S(1)}, u32[]{:S(2)}, u32[]{:S(2)}) collective-permute-start(f32[96,128]{1,0:T(8,128)S(1)} %reduce_sum.9.mine_ref), channel_id=1, source_target_pairs={{0,128},{16,144},{32,160},{48,176},{64,192},{80,208},{96,224},{112... | collective-permute-start | bytes 147464 | tf_op jit(solution)/shard_map/ppermute | solution.py:117
  22.0 14.0 %all-to-all-start.2 = ((f32[8,2,8,256]{3,2,1,0:T(8,128)}), f32[8,2,8,256]{3,2,1,0:T(8,128)S(1)}, u32[]{:S(2)}, u32[]{:S(2)}) async-start(f32[8,2,8,256]{3,2,1,0:T(8,128)} %get-tuple-element.16), calls=%async_computation.2 | async-start | bytes 262144 | tf_op jit(solution)/shard_map/all_to_all | solution.py:121
  27.0 16.8 %collective-permute-start.1 = (f32[96,128]{1,0:T(8,128)S(1)}, f32[96,128]{1,0:T(8,128)S(1)}, u32[]{:S(2)}, u32[]{:S(2)}) collective-permute-start(f32[96,128]{1,0:T(8,128)S(1)} %pair_sum.1.mine_ref), channel_id=1, source_target_pairs={{0,256},{16,272},{32,288},{48,304},{64,320},{80,336},{96,352},{112... | collective-permute-start | bytes 147464 | tf_op jit(solution)/shard_map/ppermute | solution.py:117
  36.1 12.5 %collective-permute-start.2 = (f32[8,256]{1,0:T(8,128)S(1)}, f32[8,256]{1,0:T(8,128)S(1)}, u32[]{:S(2)}, u32[]{:S(2)}) collective-permute-start(f32[8,256]{1,0:T(8,128)S(1)} %get-tuple-element.19), channel_id=1, source_target_pairs={{0,130},{1,131},{2,128},{3,129},{4,134},{5,135},{6,132},{7,133},{8... | collective-permute-start | bytes 24584 | tf_op jit(solution)/shard_map/ppermute | solution.py:179
  44.6 11.7 %all-to-all-start.1 = ((f32[8,96,128]{2,1,0:T(8,128)}), f32[8,96,128]{2,1,0:T(8,128)S(1)}, u32[]{:S(2)}, u32[]{:S(2)}) async-start(f32[8,96,128]{2,1,0:T(8,128)} %spread.1), calls=%async_computation.1 | async-start | bytes 786432 | tf_op jit(solution)/shard_map/all_to_all | solution.py:121
  48.0 8.2 %copy-start = (f32[32,3072]{1,0:T(8,128)S(1)}, f32[32,3072]{1,0:T(8,128)}, u32[]{:S(2)}) copy-start(f32[32,3072]{1,0:T(8,128)} %params_ref.1) | copy-start | bytes 1179652
  48.0 8.2 %copy-start.1 = (f32[1,3072]{1,0:T(1,128)S(1)}, f32[1,3072]{1,0:T(1,128)}, u32[]{:S(2)}) copy-start(f32[1,3072]{1,0:T(1,128)} %moment_ref.3) | copy-start | bytes 36868
  48.6 6.4 %collective-permute-start.3 = (f32[8,256]{1,0:T(8,128)S(1)}, f32[8,256]{1,0:T(8,128)S(1)}, u32[]{:S(2)}, u32[]{:S(2)}) collective-permute-start(f32[8,256]{1,0:T(8,128)S(1)} %relay.1), channel_id=1, source_target_pairs={{0,128},{16,144},{32,160},{48,176},{64,192},{80,208},{96,224},{112... | collective-permute-start | bytes 24584 | tf_op jit(solution)/shard_map/ppermute | solution.py:117

commit v5 on v4

--- a/solution.py
+++ b/solution.py
@@ -176,14 +176,11 @@
     keep, send = pl.pallas_call(
         side_kernel, out_shape=(part, part), compiler_params=small, name="column_sum"
     )(came)
+    places = [(i, j) for i in range(groups) for j in range(shares)]
     came = lax.ppermute(
         send,
         ("rep", "tp"),
-        [
-            (i * shares + j, (i ^ near) * shares + (j ^ 2))
-            for i in range(groups)
-            for j in range(shares)
-        ],
+        [(i * shares + j, (i ^ (near if j & 2 else 2 * near)) * shares + (j ^ 2)) for i, j in places],
     )
     moved = swap(chunk, "rep", near)
     chunk = pl.pallas_call(
@@ -207,7 +204,11 @@
         cost_estimate=pl.CostEstimate(flops=10**11, bytes_accessed=10**9, transcendentals=0),
         name="relay",
     )(came)
-    came = swap(came, "rep", near)
+    came = lax.ppermute(
+        came,
+        ("rep", "tp"),
+        [(i * shares + j, (i ^ (2 * near if j & 2 else near)) * shares + j) for i, j in places],
+    )
     sums = exchange(copies, "rep", near_groups)
     new_params, new_moment, input_grad_t = pl.pallas_call(
         finish_kernel,

time: 57.6 us -> 56.5 us (0.981)
  starting transfers between devices: 38.9 us -> 36.6 us
  waiting for transfers between devices: 8.42 us -> 9.71 us
    ppermute x1 -> x2, waiting for transfers between devices: 0.54 us -> 6.28 us  [the longest x1 4.5 us: on_device(): lax.ppermute(came, ('rep', 'tp'), [(i * shares + j, (i ^ (2 * near if j &...]
    ppermute x3 -> x2, waiting for transfers between devices: 3.43 us -> 0.01 us  [swap(): return lax.ppermute(array, axis, [(i, i ^ bit) for i in range(size)])]
    ppermute x3 -> x2, starting transfers between devices: 17.3 us -> 14.3 us  [swap(): return lax.ppermute(array, axis, [(i, i ^ bit) for i in range(size)])]
    all_to_all x3, waiting for transfers between devices: 4.45 us -> 3.43 us  [exchange(): lax.all_to_all(array, axis, 0, 0, axis_index_groups=groups, tiled=True)]
    ppermute x1 -> x2, starting transfers between devices: 7.64 us -> 8.32 us  [the longest x1 6.4 us: on_device(): lax.ppermute(send, ('rep', 'tp'), [(i * shares + j, (i ^ (near if j & 2 e...]
where the time goes in v5:
time: 56.5 us; the launch traced here: 56 us
  starting transfers between devices  36.6 us (65%)
  waiting for transfers between devices  9.71 us (17%)
  Pallas kernels  8.92 us (16%)
  between operations  0.72 us (1%)
    ppermute x2, starting transfers between devices, swap(): return lax.ppermute(array, axis, [(i, i ^ bit) for i in range(size)])  14.3 us
    all_to_all x3, starting transfers between devices, exchange(): lax.all_to_all(array, axis, 0, 0, axis_index_groups=groups, tiled=True)  14 us
    ppermute x1, starting transfers between devices, on_device(): lax.ppermute(send, ('rep', 'tp'), [(i * shares + j, (i ^ (near if j & 2 e...  6.4 us
    pallas_call x1, Pallas kernels, on_device(): pl.pallas_call(backward_kernel, grid=(hidden // tile,), in_specs=[full((t...  5.21 us
    ppermute x1, waiting for transfers between devices, on_device(): lax.ppermute(came, ('rep', 'tp'), [(i * shares + j, (i ^ (2 * near if j &...  4.5 us
    all_to_all x3, waiting for transfers between devices, exchange(): lax.all_to_all(array, axis, 0, 0, axis_index_groups=groups, tiled=True)  3.43 us
    pallas_call x1, Pallas kernels, on_device(): pl.pallas_call(functools.partial(dequant_kernel, groups=groups), out_shap...  2.06 us
    ppermute x1, starting transfers between devices, on_device(): lax.ppermute(came, ('rep', 'tp'), [(i * shares + j, (i ^ (2 * near if j &...  1.92 us
  transfers between devices with their start and end apart: 7, of which 4 were waited for; matrix products, arithmetic and copies ran while one was open for 0% of the time, Pallas kernels for 11%

profile of v5, /device:TPU:8, one launch (start us, length us, event | category | flops | bytes accessed | tf_op | source)
XLA Modules:
  0.0 56.0 jit_solution(362874213949770727)
XLA Ops:
  0.6 2.1 %dequant.1 = f32[8,96,128]{2,1,0:T(8,128)} custom-call(s32[1,32,3072]{2,1,0:T(8,128)} %codes_ref.1, f32[1,24,32]{2,1,0:T(8,128)} %bitcast.1, f32[1,3072]{1,0:T(1,128)} %moment_ref.3), custom_call_target="tpu_custom_call" | custom-call | tf_op jit(solution)/shard_map/dequant/pallas_call | solution.py:133
  2.7 5.7 %all-to-all-start = ((f32[8,96,128]{2,1,0:T(8,128)}), f32[8,96,128]{2,1,0:T(8,128)S(1)}, u32[]{:S(2)}, u32[]{:S(2)}) async-start(f32[8,96,128]{2,1,0:T(8,128)} %dequant.1), calls=%async_computation | async-start | bytes 786432 | tf_op jit(solution)/shard_map/all_to_all | solution.py:121
  8.3 5.2 %backward.1 = (bf16[1,128,3072]{2,1,0:T(8,128)(2,1)}, f32[8,2,8,256]{3,2,1,0:T(8,128)}) custom-call(bf16[256,128]{1,0:T(8,128)(2,1)} %inputs_ref, bf16[256,3072]{1,0:T(8,128)(2,1)} %pre_ref.1, bf16[256,3072]{1,0:T(8,128)(2,1)} %grad_ref.1, bf16[1,128,3072]{2,1,0:T(8,128)(2,1)} %weights_ref.1), custom_call_target="tpu_custom_call" | custom-call | flops 402653184 | bytes 4718592 | tf_op jit(solution)/shard_map/backward/pallas_call | solution.py:146
  13.6 3.2 %all-to-all-done = f32[8,96,128]{2,1,0:T(8,128)S(1)} async-done(((f32[8,96,128]{2,1,0:T(8,128)}), f32[8,96,128]{2,1,0:T(8,128)S(1)}, u32[]{:S(2)}, u32[]{:S(2)}) %all-to-all-start) | async-done | bytes 393248 | tf_op jit(solution)/shard_map/all_to_all | solution.py:121
  16.8 5.2 %collective-permute-start = (f32[96,128]{1,0:T(8,128)S(1)}, f32[96,128]{1,0:T(8,128)S(1)}, u32[]{:S(2)}, u32[]{:S(2)}) collective-permute-start(f32[96,128]{1,0:T(8,128)S(1)} %reduce_sum.9.mine_ref), channel_id=1, source_target_pairs={{0,128},{16,144},{32,160},{48,176},{64,192},{80,208},{96,224},{112... | collective-permute-start | bytes 147464 | tf_op jit(solution)/shard_map/ppermute | solution.py:117
  22.0 4.9 %all-to-all-start.2 = ((f32[8,2,8,256]{3,2,1,0:T(8,128)}), f32[8,2,8,256]{3,2,1,0:T(8,128)S(1)}, u32[]{:S(2)}, u32[]{:S(2)}) async-start(f32[8,2,8,256]{3,2,1,0:T(8,128)} %get-tuple-element.16), calls=%async_computation.2 | async-start | bytes 262144 | tf_op jit(solution)/shard_map/all_to_all | solution.py:121
  26.9 0.0 collective-permute-done.came_ref
  27.0 9.1 %collective-permute-start.1 = (f32[96,128]{1,0:T(8,128)S(1)}, f32[96,128]{1,0:T(8,128)S(1)}, u32[]{:S(2)}, u32[]{:S(2)}) collective-permute-start(f32[96,128]{1,0:T(8,128)S(1)} %pair_sum.1.mine_ref), channel_id=1, source_target_pairs={{0,256},{16,272},{32,288},{48,304},{64,320},{80,336},{96,352},{112... | collective-permute-start | bytes 147464 | tf_op jit(solution)/shard_map/ppermute | solution.py:117
  36.1 0.0 all-to-all-done.2.came_ref
  36.1 6.4 %collective-permute-start.2 = (f32[8,256]{1,0:T(8,128)S(1)}, f32[8,256]{1,0:T(8,128)S(1)}, u32[]{:S(2)}, u32[]{:S(2)}) collective-permute-start(f32[8,256]{1,0:T(8,128)S(1)} %get-tuple-element.19), channel_id=1, source_target_pairs={{0,258},{1,259},{2,128},{3,129},{4,262},{5,263},{6,132},{7,133},{8... | collective-permute-start | bytes 24584 | tf_op jit(solution)/shard_map/ppermute | solution.py:180
  42.5 0.0 collective-permute-done.1.came_ref
  42.5 0.8 %spread.1 = f32[8,96,128]{2,1,0:T(8,128)} custom-call(f32[96,128]{1,0:T(8,128)S(1)} %pair_sum.1.mine_ref, f32[96,128]{1,0:T(8,128)S(1)} %collective-permute-done.1.came_ref), custom_call_target="tpu_custom_call" | custom-call | tf_op jit(solution)/shard_map/spread/pallas_call | solution.py:194
  43.3 3.5 %all-to-all-start.1 = ((f32[8,96,128]{2,1,0:T(8,128)}), f32[8,96,128]{2,1,0:T(8,128)S(1)}, u32[]{:S(2)}, u32[]{:S(2)}) async-start(f32[8,96,128]{2,1,0:T(8,128)} %spread.1), calls=%async_computation.1 | async-start | bytes 786432 | tf_op jit(solution)/shard_map/all_to_all | solution.py:121
  46.8 0.0 copy-start
  46.8 0.0 copy-start.1
  46.8 1.8 %collective-permute-done.2.came_ref = f32[8,256]{1,0:T(8,128)S(1)} collective-permute-done((f32[8,256]{1,0:T(8,128)S(1)}, f32[8,256]{1,0:T(8,128)S(1)}, u32[]{:S(2)}, u32[]{:S(2)}) %collective-permute-start.2) | collective-permute-done | bytes 8224 | tf_op jit(solution)/shard_map/ppermute | solution.py:180
  48.6 1.9 %collective-permute-start.3 = (f32[8,256]{1,0:T(8,128)S(1)}, f32[8,256]{1,0:T(8,128)S(1)}, u32[]{:S(2)}, u32[]{:S(2)}) collective-permute-start(f32[8,256]{1,0:T(8,128)S(1)} %relay.1), channel_id=1, source_target_pairs={{0,128},{1,129},{2,258},{3,259},{4,132},{5,133},{6,262},{7,263},{8... | collective-permute-start | bytes 24584 | tf_op jit(solution)/shard_map/ppermute | solution.py:207
  50.5 4.5 %collective-permute-done.3.came_ref = f32[8,256]{1,0:T(8,128)S(1)} collective-permute-done((f32[8,256]{1,0:T(8,128)S(1)}, f32[8,256]{1,0:T(8,128)S(1)}, u32[]{:S(2)}, u32[]{:S(2)}) %collective-permute-start.3) | collective-permute-done | bytes 8224 | tf_op jit(solution)/shard_map/ppermute | solution.py:207
  55.0 0.2 all-to-all-done.1.sums_ref
  55.2 0.0 copy-done
  55.2 0.0 copy-done.1
  55.2 0.8 %finish.1 = (f32[32,3072]{1,0:T(8,128)}, f32[1,3072]{1,0:T(1,128)}, bf16[8,256]{1,0:T(8,128)(2,1)}) custom-call(f32[8,96,128]{2,1,0:T(8,128)S(1)} %all-to-all-done.1.sums_ref, f32[32,3072]{1,0:T(8,128)S(1)} %copy-done, f32[1,3072]{1,0:T(1,128)S(1)} %copy-done.1, f32[8,256]{1,0:T(8,128)S(1)} %get-tuple-element.18.kept_ref, ...), custom_call_target="tpu_custom_call" | custom-call | tf_op jit(solution)/shard_map/finish/pallas_call | solution.py:213
  (4 shorter events, 0.1 us)
Async XLA Ops:
  2.7 14.1 %all-to-all-start = ((f32[8,96,128]{2,1,0:T(8,128)}), f32[8,96,128]{2,1,0:T(8,128)S(1)}, u32[]{:S(2)}, u32[]{:S(2)}) async-start(f32[8,96,128]{2,1,0:T(8,128)} %dequant.1), calls=%async_computation | async-start | bytes 786432 | tf_op jit(solution)/shard_map/all_to_all | solution.py:121
  16.8 10.1 %collective-permute-start = (f32[96,128]{1,0:T(8,128)S(1)}, f32[96,128]{1,0:T(8,128)S(1)}, u32[]{:S(2)}, u32[]{:S(2)}) collective-permute-start(f32[96,128]{1,0:T(8,128)S(1)} %reduce_sum.9.mine_ref), channel_id=1, source_target_pairs={{0,128},{16,144},{32,160},{48,176},{64,192},{80,208},{96,224},{112... | collective-permute-start | bytes 147464 | tf_op jit(solution)/shard_map/ppermute | solution.py:117
  22.0 14.0 %all-to-all-start.2 = ((f32[8,2,8,256]{3,2,1,0:T(8,128)}), f32[8,2,8,256]{3,2,1,0:T(8,128)S(1)}, u32[]{:S(2)}, u32[]{:S(2)}) async-start(f32[8,2,8,256]{3,2,1,0:T(8,128)} %get-tuple-element.16), calls=%async_computation.2 | async-start | bytes 262144 | tf_op jit(solution)/shard_map/all_to_all | solution.py:121
  27.0 15.6 %collective-permute-start.1 = (f32[96,128]{1,0:T(8,128)S(1)}, f32[96,128]{1,0:T(8,128)S(1)}, u32[]{:S(2)}, u32[]{:S(2)}) collective-permute-start(f32[96,128]{1,0:T(8,128)S(1)} %pair_sum.1.mine_ref), channel_id=1, source_target_pairs={{0,256},{16,272},{32,288},{48,304},{64,320},{80,336},{96,352},{112... | collective-permute-start | bytes 147464 | tf_op jit(solution)/shard_map/ppermute | solution.py:117
  36.1 12.5 %collective-permute-start.2 = (f32[8,256]{1,0:T(8,128)S(1)}, f32[8,256]{1,0:T(8,128)S(1)}, u32[]{:S(2)}, u32[]{:S(2)}) collective-permute-start(f32[8,256]{1,0:T(8,128)S(1)} %get-tuple-element.19), channel_id=1, source_target_pairs={{0,258},{1,259},{2,128},{3,129},{4,262},{5,263},{6,132},{7,133},{8... | collective-permute-start | bytes 24584 | tf_op jit(solution)/shard_map/ppermute | solution.py:180
  43.3 11.9 %all-to-all-start.1 = ((f32[8,96,128]{2,1,0:T(8,128)}), f32[8,96,128]{2,1,0:T(8,128)S(1)}, u32[]{:S(2)}, u32[]{:S(2)}) async-start(f32[8,96,128]{2,1,0:T(8,128)} %spread.1), calls=%async_computation.1 | async-start | bytes 786432 | tf_op jit(solution)/shard_map/all_to_all | solution.py:121
  46.8 8.4 %copy-start = (f32[32,3072]{1,0:T(8,128)S(1)}, f32[32,3072]{1,0:T(8,128)}, u32[]{:S(2)}) copy-start(f32[32,3072]{1,0:T(8,128)} %params_ref.1) | copy-start | bytes 1179652
  46.8 8.4 %copy-start.1 = (f32[1,3072]{1,0:T(1,128)S(1)}, f32[1,3072]{1,0:T(1,128)}, u32[]{:S(2)}) copy-start(f32[1,3072]{1,0:T(1,128)} %moment_ref.3) | copy-start | bytes 36868
  48.6 6.4 %collective-permute-start.3 = (f32[8,256]{1,0:T(8,128)S(1)}, f32[8,256]{1,0:T(8,128)S(1)}, u32[]{:S(2)}, u32[]{:S(2)}) collective-permute-start(f32[8,256]{1,0:T(8,128)S(1)} %relay.1), channel_id=1, source_target_pairs={{0,128},{1,129},{2,258},{3,259},{4,132},{5,133},{6,262},{7,263},{8... | collective-permute-start | bytes 24584 | tf_op jit(solution)/shard_map/ppermute | solution.py:207

commit v6 on v5

--- a/solution.py
+++ b/solution.py
@@ -180,7 +180,7 @@
     came = lax.ppermute(
         send,
         ("rep", "tp"),
-        [(i * shares + j, (i ^ (near if j & 2 else 2 * near)) * shares + (j ^ 2)) for i, j in places],
+        [(i * shares + j, (i ^ (near if j & 2 else 3 * near)) * shares + (j ^ 2)) for i, j in places],
     )
     moved = swap(chunk, "rep", near)
     chunk = pl.pallas_call(
@@ -207,7 +207,7 @@
     came = lax.ppermute(
         came,
         ("rep", "tp"),
-        [(i * shares + j, (i ^ (2 * near if j & 2 else near)) * shares + j) for i, j in places],
+        [(i * shares + j, (i ^ (3 * near if j & 2 else near)) * shares + j) for i, j in places],
     )
     sums = exchange(copies, "rep", near_groups)
     new_params, new_moment, input_grad_t = pl.pallas_call(

time: 56.5 us -> 56.4 us (level)
    ppermute x1, starting transfers between devices: 6.4 us -> 5.49 us  [on_device(): lax.ppermute(send, ('rep', 'tp'), [(i * shares + j, (i ^ (near if j & 2 e...]
    ppermute x1, waiting for transfers between devices: 1.78 us -> 2.69 us  [on_device(): lax.ppermute(send, ('rep', 'tp'), [(i * shares + j, (i ^ (near if j & 2 e...]
    ppermute x1, starting transfers between devices: 1.92 us -> 2.64 us  [on_device(): lax.ppermute(came, ('rep', 'tp'), [(i * shares + j, (i ^ (3 * near if j &...]
    ppermute x1, waiting for transfers between devices: 4.5 us -> 3.78 us  [on_device(): lax.ppermute(came, ('rep', 'tp'), [(i * shares + j, (i ^ (3 * near if j &...]
  transfers between devices with their start and end apart: 7 -> 7, of which waited for: 4 -> 3; matrix products, arithmetic and copies ran while one was open for 0% -> 0% of each run, Pallas kernels for 11% -> 11%
where the time goes in v6:
time: 56.4 us; the launch traced here: 55.9 us
  starting transfers between devices  36.4 us (65%)
  waiting for transfers between devices  9.73 us (17%)
  Pallas kernels  8.92 us (16%)
  between operations  0.72 us (1%)
    ppermute x2, starting transfers between devices, swap(): return lax.ppermute(array, axis, [(i, i ^ bit) for i in range(size)])  14.3 us
    all_to_all x3, starting transfers between devices, exchange(): lax.all_to_all(array, axis, 0, 0, axis_index_groups=groups, tiled=True)  14 us
    ppermute x1, starting transfers between devices, on_device(): lax.ppermute(send, ('rep', 'tp'), [(i * shares + j, (i ^ (near if j & 2 e...  5.49 us
    pallas_call x1, Pallas kernels, on_device(): pl.pallas_call(backward_kernel, grid=(hidden // tile,), in_specs=[full((t...  5.21 us
    ppermute x1, waiting for transfers between devices, on_device(): lax.ppermute(came, ('rep', 'tp'), [(i * shares + j, (i ^ (3 * near if j &...  3.78 us
    all_to_all x3, waiting for transfers between devices, exchange(): lax.all_to_all(array, axis, 0, 0, axis_index_groups=groups, tiled=True)  3.25 us
    ppermute x1, waiting for transfers between devices, on_device(): lax.ppermute(send, ('rep', 'tp'), [(i * shares + j, (i ^ (near if j & 2 e...  2.69 us
    ppermute x1, starting transfers between devices, on_device(): lax.ppermute(came, ('rep', 'tp'), [(i * shares + j, (i ^ (3 * near if j &...  2.64 us
  transfers between devices with their start and end apart: 7, of which 3 were waited for; matrix products, arithmetic and copies ran while one was open for 0% of the time, Pallas kernels for 11%

profile of v6, /device:TPU:8, one launch (start us, length us, event | category | flops | bytes accessed | tf_op | source)
XLA Modules:
  0.0 55.9 jit_solution(382066643327939987)
XLA Ops:
  0.6 2.1 %dequant.1 = f32[8,96,128]{2,1,0:T(8,128)} custom-call(s32[1,32,3072]{2,1,0:T(8,128)} %codes_ref.1, f32[1,24,32]{2,1,0:T(8,128)} %bitcast.1, f32[1,3072]{1,0:T(1,128)} %moment_ref.3), custom_call_target="tpu_custom_call" | custom-call | tf_op jit(solution)/shard_map/dequant/pallas_call | solution.py:133
  2.7 5.7 %all-to-all-start = ((f32[8,96,128]{2,1,0:T(8,128)}), f32[8,96,128]{2,1,0:T(8,128)S(1)}, u32[]{:S(2)}, u32[]{:S(2)}) async-start(f32[8,96,128]{2,1,0:T(8,128)} %dequant.1), calls=%async_computation | async-start | bytes 786432 | tf_op jit(solution)/shard_map/all_to_all | solution.py:121
  8.3 5.2 %backward.1 = (bf16[1,128,3072]{2,1,0:T(8,128)(2,1)}, f32[8,2,8,256]{3,2,1,0:T(8,128)}) custom-call(bf16[256,128]{1,0:T(8,128)(2,1)} %inputs_ref, bf16[256,3072]{1,0:T(8,128)(2,1)} %pre_ref.1, bf16[256,3072]{1,0:T(8,128)(2,1)} %grad_ref.1, bf16[1,128,3072]{2,1,0:T(8,128)(2,1)} %weights_ref.1), custom_call_target="tpu_custom_call" | custom-call | flops 402653184 | bytes 4718592 | tf_op jit(solution)/shard_map/backward/pallas_call | solution.py:146
  13.6 3.2 %all-to-all-done = f32[8,96,128]{2,1,0:T(8,128)S(1)} async-done(((f32[8,96,128]{2,1,0:T(8,128)}), f32[8,96,128]{2,1,0:T(8,128)S(1)}, u32[]{:S(2)}, u32[]{:S(2)}) %all-to-all-start) | async-done | bytes 393248 | tf_op jit(solution)/shard_map/all_to_all | solution.py:121
  16.8 5.2 %collective-permute-start = (f32[96,128]{1,0:T(8,128)S(1)}, f32[96,128]{1,0:T(8,128)S(1)}, u32[]{:S(2)}, u32[]{:S(2)}) collective-permute-start(f32[96,128]{1,0:T(8,128)S(1)} %reduce_sum.9.mine_ref), channel_id=1, source_target_pairs={{0,128},{16,144},{32,160},{48,176},{64,192},{80,208},{96,224},{112... | collective-permute-start | bytes 147464 | tf_op jit(solution)/shard_map/ppermute | solution.py:117
  22.0 4.9 %all-to-all-start.2 = ((f32[8,2,8,256]{3,2,1,0:T(8,128)}), f32[8,2,8,256]{3,2,1,0:T(8,128)S(1)}, u32[]{:S(2)}, u32[]{:S(2)}) async-start(f32[8,2,8,256]{3,2,1,0:T(8,128)} %get-tuple-element.16), calls=%async_computation.2 | async-start | bytes 262144 | tf_op jit(solution)/shard_map/all_to_all | solution.py:121
  26.9 0.0 collective-permute-done.came_ref
  27.0 9.1 %collective-permute-start.1 = (f32[96,128]{1,0:T(8,128)S(1)}, f32[96,128]{1,0:T(8,128)S(1)}, u32[]{:S(2)}, u32[]{:S(2)}) collective-permute-start(f32[96,128]{1,0:T(8,128)S(1)} %pair_sum.1.mine_ref), channel_id=1, source_target_pairs={{0,256},{16,272},{32,288},{48,304},{64,320},{80,336},{96,352},{112... | collective-permute-start | bytes 147464 | tf_op jit(solution)/shard_map/ppermute | solution.py:117
  36.1 0.0 all-to-all-done.2.came_ref
  36.1 5.5 %collective-permute-start.2 = (f32[8,256]{1,0:T(8,128)S(1)}, f32[8,256]{1,0:T(8,128)S(1)}, u32[]{:S(2)}, u32[]{:S(2)}) collective-permute-start(f32[8,256]{1,0:T(8,128)S(1)} %get-tuple-element.19), channel_id=1, source_target_pairs={{0,386},{1,387},{2,128},{3,129},{4,390},{5,391},{6,132},{7,133},{8... | collective-permute-start | bytes 24584 | tf_op jit(solution)/shard_map/ppermute | solution.py:180
  41.6 0.0 collective-permute-done.1.came_ref
  41.6 0.8 %spread.1 = f32[8,96,128]{2,1,0:T(8,128)} custom-call(f32[96,128]{1,0:T(8,128)S(1)} %pair_sum.1.mine_ref, f32[96,128]{1,0:T(8,128)S(1)} %collective-permute-done.1.came_ref), custom_call_target="tpu_custom_call" | custom-call | tf_op jit(solution)/shard_map/spread/pallas_call | solution.py:194
  42.4 3.5 %all-to-all-start.1 = ((f32[8,96,128]{2,1,0:T(8,128)}), f32[8,96,128]{2,1,0:T(8,128)S(1)}, u32[]{:S(2)}, u32[]{:S(2)}) async-start(f32[8,96,128]{2,1,0:T(8,128)} %spread.1), calls=%async_computation.1 | async-start | bytes 786432 | tf_op jit(solution)/shard_map/all_to_all | solution.py:121
  45.9 0.0 copy-start
  45.9 0.0 copy-start.1
  45.9 2.7 %collective-permute-done.2.came_ref = f32[8,256]{1,0:T(8,128)S(1)} collective-permute-done((f32[8,256]{1,0:T(8,128)S(1)}, f32[8,256]{1,0:T(8,128)S(1)}, u32[]{:S(2)}, u32[]{:S(2)}) %collective-permute-start.2) | collective-permute-done | bytes 8224 | tf_op jit(solution)/shard_map/ppermute | solution.py:180
  48.6 2.6 %collective-permute-start.3 = (f32[8,256]{1,0:T(8,128)S(1)}, f32[8,256]{1,0:T(8,128)S(1)}, u32[]{:S(2)}, u32[]{:S(2)}) collective-permute-start(f32[8,256]{1,0:T(8,128)S(1)} %relay.1), channel_id=1, source_target_pairs={{0,128},{1,129},{2,386},{3,387},{4,132},{5,133},{6,390},{7,391},{8... | collective-permute-start | bytes 24584 | tf_op jit(solution)/shard_map/ppermute | solution.py:207
  51.2 3.8 %collective-permute-done.3.came_ref = f32[8,256]{1,0:T(8,128)S(1)} collective-permute-done((f32[8,256]{1,0:T(8,128)S(1)}, f32[8,256]{1,0:T(8,128)S(1)}, u32[]{:S(2)}, u32[]{:S(2)}) %collective-permute-start.3) | collective-permute-done | bytes 8224 | tf_op jit(solution)/shard_map/ppermute | solution.py:207
  55.0 0.0 all-to-all-done.1.sums_ref
  55.0 0.0 copy-done
  55.0 0.0 copy-done.1
  55.0 0.8 %finish.1 = (f32[32,3072]{1,0:T(8,128)}, f32[1,3072]{1,0:T(1,128)}, bf16[8,256]{1,0:T(8,128)(2,1)}) custom-call(f32[8,96,128]{2,1,0:T(8,128)S(1)} %all-to-all-done.1.sums_ref, f32[32,3072]{1,0:T(8,128)S(1)} %copy-done, f32[1,3072]{1,0:T(1,128)S(1)} %copy-done.1, f32[8,256]{1,0:T(8,128)S(1)} %get-tuple-element.18.kept_ref, ...), custom_call_target="tpu_custom_call" | custom-call | tf_op jit(solution)/shard_map/finish/pallas_call | solution.py:213
  (4 shorter events, 0.1 us)
Async XLA Ops:
  2.7 14.1 %all-to-all-start = ((f32[8,96,128]{2,1,0:T(8,128)}), f32[8,96,128]{2,1,0:T(8,128)S(1)}, u32[]{:S(2)}, u32[]{:S(2)}) async-start(f32[8,96,128]{2,1,0:T(8,128)} %dequant.1), calls=%async_computation | async-start | bytes 786432 | tf_op jit(solution)/shard_map/all_to_all | solution.py:121
  16.8 10.1 %collective-permute-start = (f32[96,128]{1,0:T(8,128)S(1)}, f32[96,128]{1,0:T(8,128)S(1)}, u32[]{:S(2)}, u32[]{:S(2)}) collective-permute-start(f32[96,128]{1,0:T(8,128)S(1)} %reduce_sum.9.mine_ref), channel_id=1, source_target_pairs={{0,128},{16,144},{32,160},{48,176},{64,192},{80,208},{96,224},{112... | collective-permute-start | bytes 147464 | tf_op jit(solution)/shard_map/ppermute | solution.py:117
  22.0 14.0 %all-to-all-start.2 = ((f32[8,2,8,256]{3,2,1,0:T(8,128)}), f32[8,2,8,256]{3,2,1,0:T(8,128)S(1)}, u32[]{:S(2)}, u32[]{:S(2)}) async-start(f32[8,2,8,256]{3,2,1,0:T(8,128)} %get-tuple-element.16), calls=%async_computation.2 | async-start | bytes 262144 | tf_op jit(solution)/shard_map/all_to_all | solution.py:121
  27.0 14.7 %collective-permute-start.1 = (f32[96,128]{1,0:T(8,128)S(1)}, f32[96,128]{1,0:T(8,128)S(1)}, u32[]{:S(2)}, u32[]{:S(2)}) collective-permute-start(f32[96,128]{1,0:T(8,128)S(1)} %pair_sum.1.mine_ref), channel_id=1, source_target_pairs={{0,256},{16,272},{32,288},{48,304},{64,320},{80,336},{96,352},{112... | collective-permute-start | bytes 147464 | tf_op jit(solution)/shard_map/ppermute | solution.py:117
  36.1 12.5 %collective-permute-start.2 = (f32[8,256]{1,0:T(8,128)S(1)}, f32[8,256]{1,0:T(8,128)S(1)}, u32[]{:S(2)}, u32[]{:S(2)}) collective-permute-start(f32[8,256]{1,0:T(8,128)S(1)} %get-tuple-element.19), channel_id=1, source_target_pairs={{0,386},{1,387},{2,128},{3,129},{4,390},{5,391},{6,132},{7,133},{8... | collective-permute-start | bytes 24584 | tf_op jit(solution)/shard_map/ppermute | solution.py:180
  42.4 12.6 %all-to-all-start.1 = ((f32[8,96,128]{2,1,0:T(8,128)}), f32[8,96,128]{2,1,0:T(8,128)S(1)}, u32[]{:S(2)}, u32[]{:S(2)}) async-start(f32[8,96,128]{2,1,0:T(8,128)} %spread.1), calls=%async_computation.1 | async-start | bytes 786432 | tf_op jit(solution)/shard_map/all_to_all | solution.py:121
  45.9 9.2 %copy-start = (f32[32,3072]{1,0:T(8,128)S(1)}, f32[32,3072]{1,0:T(8,128)}, u32[]{:S(2)}) copy-start(f32[32,3072]{1,0:T(8,128)} %params_ref.1) | copy-start | bytes 1179652
  45.9 9.1 %copy-start.1 = (f32[1,3072]{1,0:T(1,128)S(1)}, f32[1,3072]{1,0:T(1,128)}, u32[]{:S(2)}) copy-start(f32[1,3072]{1,0:T(1,128)} %moment_ref.3) | copy-start | bytes 36868
  48.6 6.4 %collective-permute-start.3 = (f32[8,256]{1,0:T(8,128)S(1)}, f32[8,256]{1,0:T(8,128)S(1)}, u32[]{:S(2)}, u32[]{:S(2)}) collective-permute-start(f32[8,256]{1,0:T(8,128)S(1)} %relay.1), channel_id=1, source_target_pairs={{0,128},{1,129},{2,386},{3,387},{4,132},{5,133},{6,390},{7,391},{8... | collective-permute-start | bytes 24584 | tf_op jit(solution)/shard_map/ppermute | solution.py:207

commit v7 on v6

--- a/solution.py
+++ b/solution.py
@@ -79,8 +79,10 @@
     out_ref[...] = mine_ref[...] + came_ref[...]
 
 
-def relay_kernel(came_ref, out_ref):
+def relay_kernel(kept_ref, came_ref, sum_ref, out_ref):
     out_ref[...] = came_ref[...]
+    upper = (lax.axis_index("tp") // 2) % 2
+    sum_ref[...] = kept_ref[...] + jnp.where(upper == 0, came_ref[...], 0.0)
 
 
 def spread_kernel(mine_ref, came_ref, copies_ref):
@@ -180,7 +182,7 @@
     came = lax.ppermute(
         send,
         ("rep", "tp"),
-        [(i * shares + j, (i ^ (near if j & 2 else 3 * near)) * shares + (j ^ 2)) for i, j in places],
+        [(i * shares + j, (i if j & 2 else i ^ (3 * near)) * shares + (j ^ 2)) for i, j in places],
     )
     moved = swap(chunk, "rep", near)
     chunk = pl.pallas_call(
@@ -197,17 +199,17 @@
         compiler_params=small,
         name="spread",
     )(chunk, moved)
-    came = pl.pallas_call(
+    keep, came = pl.pallas_call(
         relay_kernel,
-        out_shape=part,
+        out_shape=(part, part),
         compiler_params=small,
         cost_estimate=pl.CostEstimate(flops=10**11, bytes_accessed=10**9, transcendentals=0),
         name="relay",
-    )(came)
+    )(keep, came)
     came = lax.ppermute(
         came,
         ("rep", "tp"),
-        [(i * shares + j, (i ^ (3 * near if j & 2 else near)) * shares + j) for i, j in places],
+        [(i * shares + j, (i ^ (3 * near)) * shares + j) for i, j in places if j & 2],
     )
     sums = exchange(copies, "rep", near_groups)
     new_params, new_moment, input_grad_t = pl.pallas_call(

time: 56.4 us -> 55.6 us (0.986)
  starting transfers between devices: 36.4 us -> 34.6 us
  waiting for transfers between devices: 9.73 us -> 10.8 us
    all_to_all x3, waiting for transfers between devices: 3.25 us -> 6.32 us  [exchange(): lax.all_to_all(array, axis, 0, 0, axis_index_groups=groups, tiled=True)]
    ppermute x2, waiting for transfers between devices: 6.47 us -> 4.51 us  [the longest x1 4.51 us: on_device(): lax.ppermute(send, ('rep', 'tp'), [(i * shares + j, (i if j & 2 else i ^...]
    ppermute x2, starting transfers between devices: 8.13 us -> 6.28 us  [the longest x1 5.49 us: on_device(): lax.ppermute(send, ('rep', 'tp'), [(i * shares + j, (i if j & 2 else i ^...]
where the time goes in v7:
time: 55.6 us; the launch traced here: 55.1 us
  starting transfers between devices  34.6 us (62%)
  waiting for transfers between devices  10.8 us (19%)
  Pallas kernels  8.92 us (16%)
  between operations  0.72 us (1%)
    ppermute x2, starting transfers between devices, swap(): return lax.ppermute(array, axis, [(i, i ^ bit) for i in range(size)])  14.3 us
    all_to_all x3, starting transfers between devices, exchange(): lax.all_to_all(array, axis, 0, 0, axis_index_groups=groups, tiled=True)  14 us
    all_to_all x3, waiting for transfers between devices, exchange(): lax.all_to_all(array, axis, 0, 0, axis_index_groups=groups, tiled=True)  6.32 us
    ppermute x1, starting transfers between devices, on_device(): lax.ppermute(send, ('rep', 'tp'), [(i * shares + j, (i if j & 2 else i ^...  5.49 us
    pallas_call x1, Pallas kernels, on_device(): pl.pallas_call(backward_kernel, grid=(hidden // tile,), in_specs=[full((t...  5.22 us
    ppermute x1, waiting for transfers between devices, on_device(): lax.ppermute(send, ('rep', 'tp'), [(i * shares + j, (i if j & 2 else i ^...  4.51 us
    pallas_call x1, Pallas kernels, on_device(): pl.pallas_call(functools.partial(dequant_kernel, groups=groups), out_shap...  2.06 us
  transfers between devices with their start and end apart: 7, of which 3 were waited for; matrix products, arithmetic and copies ran while one was open for 0% of the time, Pallas kernels for 11%

profile of v7, /device:TPU:8, one launch (start us, length us, event | category | flops | bytes accessed | tf_op | source)
XLA Modules:
  0.0 55.1 jit_solution(7186417530059056294)
XLA Ops:
  0.6 2.1 %dequant.1 = f32[8,96,128]{2,1,0:T(8,128)} custom-call(s32[1,32,3072]{2,1,0:T(8,128)} %codes_ref.1, f32[1,24,32]{2,1,0:T(8,128)} %bitcast.1, f32[1,3072]{1,0:T(1,128)} %moment_ref.3), custom_call_target="tpu_custom_call" | custom-call | tf_op jit(solution)/shard_map/dequant/pallas_call | solution.py:135
  2.7 5.7 %all-to-all-start = ((f32[8,96,128]{2,1,0:T(8,128)}), f32[8,96,128]{2,1,0:T(8,128)S(1)}, u32[]{:S(2)}, u32[]{:S(2)}) async-start(f32[8,96,128]{2,1,0:T(8,128)} %dequant.1), calls=%async_computation | async-start | bytes 786432 | tf_op jit(solution)/shard_map/all_to_all | solution.py:123
  8.3 5.2 %backward.1 = (bf16[1,128,3072]{2,1,0:T(8,128)(2,1)}, f32[8,2,8,256]{3,2,1,0:T(8,128)}) custom-call(bf16[256,128]{1,0:T(8,128)(2,1)} %inputs_ref, bf16[256,3072]{1,0:T(8,128)(2,1)} %pre_ref.1, bf16[256,3072]{1,0:T(8,128)(2,1)} %grad_ref.1, bf16[1,128,3072]{2,1,0:T(8,128)(2,1)} %weights_ref.1), custom_call_target="tpu_custom_call" | custom-call | flops 402653184 | bytes 4718592 | tf_op jit(solution)/shard_map/backward/pallas_call | solution.py:148
  13.6 3.2 %all-to-all-done = f32[8,96,128]{2,1,0:T(8,128)S(1)} async-done(((f32[8,96,128]{2,1,0:T(8,128)}), f32[8,96,128]{2,1,0:T(8,128)S(1)}, u32[]{:S(2)}, u32[]{:S(2)}) %all-to-all-start) | async-done | bytes 393248 | tf_op jit(solution)/shard_map/all_to_all | solution.py:123
  16.8 5.2 %collective-permute-start = (f32[96,128]{1,0:T(8,128)S(1)}, f32[96,128]{1,0:T(8,128)S(1)}, u32[]{:S(2)}, u32[]{:S(2)}) collective-permute-start(f32[96,128]{1,0:T(8,128)S(1)} %reduce_sum.9.mine_ref), channel_id=1, source_target_pairs={{0,128},{16,144},{32,160},{48,176},{64,192},{80,208},{96,224},{112... | collective-permute-start | bytes 147464 | tf_op jit(solution)/shard_map/ppermute | solution.py:119
  22.0 4.9 %all-to-all-start.2 = ((f32[8,2,8,256]{3,2,1,0:T(8,128)}), f32[8,2,8,256]{3,2,1,0:T(8,128)S(1)}, u32[]{:S(2)}, u32[]{:S(2)}) async-start(f32[8,2,8,256]{3,2,1,0:T(8,128)} %get-tuple-element.18), calls=%async_computation.2 | async-start | bytes 262144 | tf_op jit(solution)/shard_map/all_to_all | solution.py:123
  26.9 0.0 collective-permute-done.came_ref
  27.0 9.1 %collective-permute-start.1 = (f32[96,128]{1,0:T(8,128)S(1)}, f32[96,128]{1,0:T(8,128)S(1)}, u32[]{:S(2)}, u32[]{:S(2)}) collective-permute-start(f32[96,128]{1,0:T(8,128)S(1)} %pair_sum.1.mine_ref), channel_id=1, source_target_pairs={{0,256},{16,272},{32,288},{48,304},{64,320},{80,336},{96,352},{112... | collective-permute-start | bytes 147464 | tf_op jit(solution)/shard_map/ppermute | solution.py:119
  36.1 0.0 all-to-all-done.2.came_ref
  36.1 5.5 %collective-permute-start.2 = (f32[8,256]{1,0:T(8,128)S(1)}, f32[8,256]{1,0:T(8,128)S(1)}, u32[]{:S(2)}, u32[]{:S(2)}) collective-permute-start(f32[8,256]{1,0:T(8,128)S(1)} %get-tuple-element.21), channel_id=1, source_target_pairs={{0,386},{1,387},{2,0},{3,1},{4,390},{5,391},{6,4},{7,5},{8,394},{9... | collective-permute-start | bytes 24584 | tf_op jit(solution)/shard_map/ppermute | solution.py:182
  41.6 0.0 collective-permute-done.1.came_ref
  41.6 0.8 %spread.1 = f32[8,96,128]{2,1,0:T(8,128)} custom-call(f32[96,128]{1,0:T(8,128)S(1)} %pair_sum.1.mine_ref, f32[96,128]{1,0:T(8,128)S(1)} %collective-permute-done.1.came_ref), custom_call_target="tpu_custom_call" | custom-call | tf_op jit(solution)/shard_map/spread/pallas_call | solution.py:196
  42.4 3.5 %all-to-all-start.1 = ((f32[8,96,128]{2,1,0:T(8,128)}), f32[8,96,128]{2,1,0:T(8,128)S(1)}, u32[]{:S(2)}, u32[]{:S(2)}) async-start(f32[8,96,128]{2,1,0:T(8,128)} %spread.1), calls=%async_computation.1 | async-start | bytes 786432 | tf_op jit(solution)/shard_map/all_to_all | solution.py:123
  45.9 4.5 %collective-permute-done.2.came_ref = f32[8,256]{1,0:T(8,128)S(1)} collective-permute-done((f32[8,256]{1,0:T(8,128)S(1)}, f32[8,256]{1,0:T(8,128)S(1)}, u32[]{:S(2)}, u32[]{:S(2)}) %collective-permute-start.2) | collective-permute-done | bytes 8224 | tf_op jit(solution)/shard_map/ppermute | solution.py:182
  50.4 0.0 copy-start
  50.4 0.0 copy-start.1
  50.4 0.8 %collective-permute-start.3 = (f32[8,256]{1,0:T(8,128)S(1)}, f32[8,256]{1,0:T(8,128)S(1)}, u32[]{:S(2)}, u32[]{:S(2)}) collective-permute-start(f32[8,256]{1,0:T(8,128)S(1)} %get-tuple-element.23), channel_id=1, source_target_pairs={{2,386},{3,387},{6,390},{7,391},{10,394},{11,395},{14,398},{15,399... | collective-permute-start | bytes 24584 | tf_op jit(solution)/shard_map/ppermute | solution.py:209
  51.2 0.0 collective-permute-done.3.came_ref
  51.2 3.1 %all-to-all-done.1.sums_ref = f32[8,96,128]{2,1,0:T(8,128)S(1)} async-done(((f32[8,96,128]{2,1,0:T(8,128)}), f32[8,96,128]{2,1,0:T(8,128)S(1)}, u32[]{:S(2)}, u32[]{:S(2)}) %all-to-all-start.1) | async-done | bytes 393248 | tf_op jit(solution)/shard_map/all_to_all | solution.py:123
  54.3 0.0 copy-done
  54.3 0.0 copy-done.1
  54.3 0.8 %finish.1 = (f32[32,3072]{1,0:T(8,128)}, f32[1,3072]{1,0:T(1,128)}, bf16[8,256]{1,0:T(8,128)(2,1)}) custom-call(f32[8,96,128]{2,1,0:T(8,128)S(1)} %all-to-all-done.1.sums_ref, f32[32,3072]{1,0:T(8,128)S(1)} %copy-done, f32[1,3072]{1,0:T(1,128)S(1)} %copy-done.1, f32[8,256]{1,0:T(8,128)S(1)} %get-tuple-element.22.kept_ref, ...), custom_call_target="tpu_custom_call" | custom-call | tf_op jit(solution)/shard_map/finish/pallas_call | solution.py:215
  (4 shorter events, 0.1 us)
Async XLA Ops:
  2.7 14.1 %all-to-all-start = ((f32[8,96,128]{2,1,0:T(8,128)}), f32[8,96,128]{2,1,0:T(8,128)S(1)}, u32[]{:S(2)}, u32[]{:S(2)}) async-start(f32[8,96,128]{2,1,0:T(8,128)} %dequant.1), calls=%async_computation | async-start | bytes 786432 | tf_op jit(solution)/shard_map/all_to_all | solution.py:123
  16.8 10.1 %collective-permute-start = (f32[96,128]{1,0:T(8,128)S(1)}, f32[96,128]{1,0:T(8,128)S(1)}, u32[]{:S(2)}, u32[]{:S(2)}) collective-permute-start(f32[96,128]{1,0:T(8,128)S(1)} %reduce_sum.9.mine_ref), channel_id=1, source_target_pairs={{0,128},{16,144},{32,160},{48,176},{64,192},{80,208},{96,224},{112... | collective-permute-start | bytes 147464 | tf_op jit(solution)/shard_map/ppermute | solution.py:119
  22.0 14.0 %all-to-all-start.2 = ((f32[8,2,8,256]{3,2,1,0:T(8,128)}), f32[8,2,8,256]{3,2,1,0:T(8,128)S(1)}, u32[]{:S(2)}, u32[]{:S(2)}) async-start(f32[8,2,8,256]{3,2,1,0:T(8,128)} %get-tuple-element.18), calls=%async_computation.2 | async-start | bytes 262144 | tf_op jit(solution)/shard_map/all_to_all | solution.py:123
  27.0 14.7 %collective-permute-start.1 = (f32[96,128]{1,0:T(8,128)S(1)}, f32[96,128]{1,0:T(8,128)S(1)}, u32[]{:S(2)}, u32[]{:S(2)}) collective-permute-start(f32[96,128]{1,0:T(8,128)S(1)} %pair_sum.1.mine_ref), channel_id=1, source_target_pairs={{0,256},{16,272},{32,288},{48,304},{64,320},{80,336},{96,352},{112... | collective-permute-start | bytes 147464 | tf_op jit(solution)/shard_map/ppermute | solution.py:119
  36.1 14.3 %collective-permute-start.2 = (f32[8,256]{1,0:T(8,128)S(1)}, f32[8,256]{1,0:T(8,128)S(1)}, u32[]{:S(2)}, u32[]{:S(2)}) collective-permute-start(f32[8,256]{1,0:T(8,128)S(1)} %get-tuple-element.21), channel_id=1, source_target_pairs={{0,386},{1,387},{2,0},{3,1},{4,390},{5,391},{6,4},{7,5},{8,394},{9... | collective-permute-start | bytes 24584 | tf_op jit(solution)/shard_map/ppermute | solution.py:182
  42.4 11.9 %all-to-all-start.1 = ((f32[8,96,128]{2,1,0:T(8,128)}), f32[8,96,128]{2,1,0:T(8,128)S(1)}, u32[]{:S(2)}, u32[]{:S(2)}) async-start(f32[8,96,128]{2,1,0:T(8,128)} %spread.1), calls=%async_computation.1 | async-start | bytes 786432 | tf_op jit(solution)/shard_map/all_to_all | solution.py:123
  50.4 3.9 %copy-start = (f32[32,3072]{1,0:T(8,128)S(1)}, f32[32,3072]{1,0:T(8,128)}, u32[]{:S(2)}) copy-start(f32[32,3072]{1,0:T(8,128)} %params_ref.1) | copy-start | bytes 1179652
  50.4 3.9 %copy-start.1 = (f32[1,3072]{1,0:T(1,128)S(1)}, f32[1,3072]{1,0:T(1,128)}, u32[]{:S(2)}) copy-start(f32[1,3072]{1,0:T(1,128)} %moment_ref.3) | copy-start | bytes 36868
  50.4 0.8 %collective-permute-start.3 = (f32[8,256]{1,0:T(8,128)S(1)}, f32[8,256]{1,0:T(8,128)S(1)}, u32[]{:S(2)}, u32[]{:S(2)}) collective-permute-start(f32[8,256]{1,0:T(8,128)S(1)} %get-tuple-element.23), channel_id=1, source_target_pairs={{2,386},{3,387},{6,390},{7,391},{10,394},{11,395},{14,398},{15,399... | collective-permute-start | bytes 24584 | tf_op jit(solution)/shard_map/ppermute | solution.py:209
